TPU v7x, 32 devices: a whole 2x2x4 slice. The times are simulated.
32 devices in a mesh: group: 2 (over x), freq: 16 (over z, y, core).
Axes of the slice: x: 2, y: 2, z: 4, core: 2. Of those that a mesh axis runs over, the one named last changes fastest.
Arguments:
- traces: bfloat16 [512, 256, 256], P(('group', 'freq')), parts along dimension 0, may hold values from -6 to 6
- velocity: bfloat16 [32, 256, 256], P(('group', 'freq')), parts along dimension 0, may hold values from 1 to 2
- poly_coef: float32 [2, 10, 4], replicated, may hold values from -0.6 to 0.6
- freq_slot: int32 [16], replicated, may hold values from 0 to 15, each once
- depth_owner: int32 [8], P('group'), parts along dimension 0, may hold values from 0 to 15, as said below
Outputs:
- depth_image: float32 [4, 512, 256], P(None, ('group', 'freq')), parts along dimension 1
- wavefield: float32 [2, 32, 256, 256], P(None, ('group', 'freq')), parts along dimension 1
There are 2 independent parts, one for each index of `group`. A program takes and returns all parts, laid end to end along the dimension named above; an argument that names none is the same for every part. Nothing has to cross between parts.
Inputs may be any that keep to these rules, and one draw needn't show every extreme that they name: `freq_slot`: each slot holds a different frequency index. `depth_owner`: the 4 entries are different.
All inputs are finite; a program needn't handle non-finite values.
Results may differ from a plain program's by a relative error of at most 0.0023.
Values may be sent and summed in bfloat16 or wider, within the bound.
No kernel may reach another device: no remote copies, remote signals or barrier semaphores. Data moves between devices by JAX's collectives and lax.ppermute only.
A program may use at most 128 MiB of HBM per device.

v0:
```python
import math

import jax
import jax.numpy as jnp
import numpy as np
from jax import lax
from jax.experimental import pallas as pl
from jax.experimental.pallas import tpu as pltpu
from jax.sharding import PartitionSpec as P

def sine_transform(size):
    index = np.arange(1, size + 1)
    matrix = np.sqrt(2.0 / (size + 1)) * np.sin(np.pi * np.outer(index, index) / (size + 1))
    return matrix, 2.0 + 2.0 * np.cos(np.pi * index / (size + 1))

def halves_of(matrix):
    high = matrix.astype(jnp.bfloat16)
    return high, (matrix - high.astype(np.float64)).astype(jnp.bfloat16)

def split(values):
    high = values.astype(jnp.bfloat16)
    return high, (values - high.astype(jnp.float32)).astype(jnp.bfloat16)

def dot(a, b):
    return jnp.dot(a, b, preferred_element_type=jnp.float32)

def factors_kernel(coef_ref, left_ref, right_ref, out_ref):
    term_count, power_count = coef_ref.shape[1:]
    block = 32
    def rows_step(i, carry):
        rows = pl.ds(pl.multiple_of(i * block, block), block)
        g = left_ref[rows, :] * right_ref[0:1, :] * 0.125 - 1.0
        twice = 2.0 * g
        sums = [[coef_ref[c, 0, j] + coef_ref[c, 1, j] * g for c in range(2)] for j in range(power_count)]
        before, now = jnp.ones_like(g), g
        for k in range(2, term_count):
            before, now = now, twice * now - before
            for j in range(power_count):
                for c in range(2):
                    sums[j][c] = sums[j][c] + coef_ref[c, k, j] * now
        for j in range(power_count):
            for c in range(2):
                out_ref[j, c, rows, :] = sums[j][c]
        return carry
    lax.fori_loop(0, left_ref.shape[0] // block, rows_step, 0)

def spectral_factors(poly_coef, nx, ny):
    _, lx = sine_transform(nx)
    _, ly = sine_transform(ny)
    left = jnp.asarray(np.broadcast_to(lx[:, None], (nx, 1)), jnp.float32)
    right = jnp.asarray(ly[None, :], jnp.float32)
    vmem = pl.BlockSpec(memory_space=pltpu.VMEM)
    return pl.pallas_call(
        factors_kernel,
        out_shape=jax.ShapeDtypeStruct((poly_coef.shape[2], 2, nx, ny), jnp.float32),
        in_specs=[pl.BlockSpec(memory_space=pltpu.SMEM), vmem, vmem],
        out_specs=vmem,
        compiler_params=pltpu.CompilerParams(vmem_limit_bytes=16 * 1024 * 1024),
        cost_estimate=pl.CostEstimate(
            flops=poly_coef.size * 2 * nx * ny, bytes_accessed=32 * nx * ny, transcendentals=0
        ),
        name="spectral_factors",
    )(poly_coef, left, right)

def depth_kernel(scale_ref, core_ref, left_ref, right_ref, factor_ref, start_ref, mine_ref, other_ref,
                 image_ref, field_ref, state, spectrum, *, image_scale):
    depth_count = image_ref.shape[0]
    power_count, _, nx, ny = factor_ref.shape
    held = mine_ref.shape[0]
    state[...] = start_ref[...]

    def along_y(values):
        high, low = split(values)
        return dot(jnp.concatenate([high, low, high], axis=1), right_ref[...])

    def along_x(values):
        high, low = split(values)
        return dot(left_ref[...], jnp.concatenate([high, high, low], axis=0))

    def depth_step(z, carry):
        for c in range(2):
            spectrum[c] = along_x(along_y(state[c]))

        def finish(ref):
            slow = scale_ref[0] / ref[z % held]
            for c in range(2):
                total = None
                for j in range(power_count - 1, -1, -1):
                    if c == 0:
                        part = factor_ref[j, 0] * spectrum[0] - factor_ref[j, 1] * spectrum[1]
                    else:
                        part = factor_ref[j, 0] * spectrum[1] + factor_ref[j, 1] * spectrum[0]
                    part = along_y(along_x(part))
                    total = part if total is None else total * slow + part
                state[c] = total

        @pl.when(z // held == core_ref[0])
        def _():
            finish(mine_ref)

        @pl.when(z // held != core_ref[0])
        def _():
            finish(other_ref)

        image_ref[z] = state[0] * image_scale
        return carry

    lax.fori_loop(0, depth_count, depth_step, 0)
    field_ref[...] = state[...]

def depth_steps(scale, core, factors, start, mine, other, depth_count, image_scale):
    _, nx, ny = start.shape
    sx, _ = sine_transform(nx)
    sy, _ = sine_transform(ny)
    xh, xl = halves_of(sx)
    yh, yl = halves_of(sy)
    left = jnp.asarray(np.concatenate([xh, xl, xh], axis=1))
    right = jnp.asarray(np.concatenate([yh, yh, yl], axis=0))
    def kernel(*refs):
        depth_kernel(*refs, image_scale=image_scale)
    smem = pl.BlockSpec(memory_space=pltpu.SMEM)
    vmem = pl.BlockSpec(memory_space=pltpu.VMEM)
    return pl.pallas_call(
        kernel,
        out_shape=(jax.ShapeDtypeStruct((depth_count, nx, ny), jnp.float32),
                   jax.ShapeDtypeStruct((2, nx, ny), jnp.float32)),
        in_specs=[smem, smem] + [vmem] * 6,
        out_specs=(vmem, vmem),
        scratch_shapes=[pltpu.VMEM((2, nx, ny), jnp.float32), pltpu.VMEM((2, nx, ny), jnp.float32)],
        compiler_params=pltpu.CompilerParams(vmem_limit_bytes=32 * 1024 * 1024),
        cost_estimate=pl.CostEstimate(
            flops=depth_count * 120 * nx * ny * (nx + ny) // 2, bytes_accessed=64 * nx * ny, transcendentals=0
        ),
        name="depth_steps",
    )(scale, core, left, right, factors, start, mine, other)


def swap_cores(array, count):
    return lax.ppermute(array, "freq", [(i, i ^ 1) for i in range(count)])


def on_device(traces, velocity, poly_coef, freq_slot, depth_owner):
    devices = lax.axis_size("freq")
    total_freq = freq_slot.shape[0]
    local_x, ny, sample_count = traces.shape
    nx = devices * local_x
    depth_count = depth_owner.shape[0]
    me = lax.axis_index("freq")
    core = me % 2

    by_rows = lax.all_to_all(
        velocity.reshape(devices, local_x, ny), "freq", split_axis=0, concat_axis=0, tiled=True
    )
    chosen = jnp.stack(
        [lax.dynamic_index_in_dim(by_rows, depth_owner[z], 0, keepdims=False) for z in range(depth_count)]
    ).astype(jnp.float16)

    freq_bin = freq_slot + 1
    sample_index = jnp.arange(sample_count, dtype=jnp.int32)
    phase_int = freq_bin[:, None] * sample_index[None, :] % sample_count
    phases = phase_int.astype(jnp.float32) * (2.0 * math.pi / sample_count)
    dft_table = (jnp.stack([jnp.cos(phases), -jnp.sin(phases)]) / math.sqrt(sample_count)).astype(
        jnp.bfloat16
    )
    spectra = jnp.einsum("cft,xyt->fcxy", dft_table, traces, preferred_element_type=jnp.float32)
    spectra = (spectra * 512.0).astype(jnp.float16)

    held = depth_count // 2
    halves = jnp.broadcast_to(
        chosen.reshape(1, 2, held, local_x, ny), (devices // 2, 2, held, local_x, ny)
    ).reshape(devices, held, local_x, ny)
    received = lax.all_to_all(
        jnp.concatenate([spectra, halves], axis=1), "freq", split_axis=0, concat_axis=0, tiled=True
    )
    gathered = received.transpose(1, 0, 2, 3).reshape(2 + held, nx, ny)
    start = gathered[:2].astype(jnp.float32) * (1.0 / 512.0)
    mine_half = gathered[2:]
    other_half = swap_cores(mine_half, devices)
    mine, other = mine_half.astype(jnp.float32), other_half.astype(jnp.float32)

    freq_value = lax.dynamic_index_in_dim(freq_bin, me, 0, keepdims=False).astype(jnp.float32)
    images, wavefield = depth_steps(
        (freq_value / total_freq).reshape(1),
        core.astype(jnp.int32).reshape(1),
        spectral_factors(poly_coef, nx, ny),
        start,
        mine,
        other,
        depth_count,
        1.0 / math.sqrt(total_freq),
    )

    by_core = images.reshape(depth_count, devices // 2, 2, local_x, ny)
    keep = lax.dynamic_index_in_dim(by_core, core, 2, keepdims=False)
    send = lax.dynamic_index_in_dim(by_core, 1 - core, 2, keepdims=False)
    pair_sum = keep + swap_cores(send, devices)
    same_core = [[i for i in range(devices) if i % 2 == c] for c in range(2)]
    shares = lax.all_to_all(
        pair_sum.transpose(1, 0, 2, 3),
        "freq",
        split_axis=0,
        concat_axis=0,
        tiled=True,
        axis_index_groups=same_core,
    )
    return (jnp.sum(shares, axis=0), wavefield[:, None])


def solution(mesh):
    return jax.shard_map(
        on_device,
        mesh=mesh,
        in_specs=(
            P(("group", "freq"), None, None),
            P(("group", "freq"), None, None),
            P(),
            P(),
            P("group"),
        ),
        out_specs=(P(None, ("group", "freq"), None), P(None, ("group", "freq"), None, None)),
        check_vma=False,
    )
```

profile of v0, /device:TPU:0, one launch (start us, length us, event | category | flops | bytes accessed | tf_op | source)
XLA Modules:
  0.0 77.4 jit_solution(6134582440728187036)
XLA Ops:
  0.6 0.0 copy-start
  0.6 7.5 %all-to-all-start = ((bf16[16,16,256]{2,1,0:T(8,128)(2,1)}), bf16[16,16,256]{2,1,0:T(8,128)(2,1)S(1)}, u32[]{:S(2)}, u32[]{:S(2)}) async-start(bf16[16,16,256]{2,1,0:T(8,128)(2,1)} %bitcast.48), calls=%async_computation | async-start | bytes 262144 | tf_op jit(solution)/shard_map/all_to_all | solution.py:151
  8.2 1.4 %fusion.25 = (s32[1]{0:T(128)}, s32[1]{0:T(128)}, s32[1]{0:T(128)}, s32[1]{0:T(128)}) fusion(s32[4]{0:T(128)} %param.13), kind=kLoop, calls=%fused_computation.36 | loop fusion | bytes 32 | tf_op jit(solution)/shard_map/slice | solution.py:155
  14.6 0.7 broadcast_add_fusion
  15.2 0.2 fusion.22
  17.9 0.7 fusion.8
  18.6 0.0 copy-start.3
  18.7 0.0 copy-start.4
  18.7 0.1 broadcast_in_dim.4
  18.9 0.1 reshape.132
  19.0 0.1 pad_maximum_fusion
  19.2 1.0 %copy.18 = f16[16,4,16,256]{3,2,1,0:T(8,128)(2,1)} copy(f16[16,4,16,256]{3,0,2,1:T(8,128)(2,1)S(1)} %pad_maximum_fusion) | data formatting | bytes 1048576 | tf_op jit(solution)/shard_map/concatenate | solution.py:173
  20.2 6.0 %all-to-all-start.1 = ((f16[16,4,16,256]{3,2,1,0:T(8,128)(2,1)}), f16[16,4,16,256]{3,2,1,0:T(8,128)(2,1)S(1)}, u32[]{:S(2)}, u32[]{:S(2)}) async-start(f16[16,4,16,256]{3,2,1,0:T(8,128)(2,1)} %copy.18), calls=%async_computation.1 | async-start | bytes 1048576 | tf_op jit(solution)/shard_map/all_to_all | solution.py:172
  26.2 0.6 dynamic_slice.24
  27.4 0.1 copy.16.coef_ref
  27.6 3.1 %spectral_factors.1.refs_4_ = f32[4,2,256,256]{3,2,1,0:T(8,128)S(1)} custom-call(f32[2,10,4]{2,1,0:T(8,128)S(1)} %copy.16.coef_ref, f32[256,1]{1,0:T(8,128)S(1)} %copy-done.3, f32[1,256]{1,0:T(1,128)S(1)} %copy-done.4), custom_call_target="tpu_custom_call" | custom-call | flops 10485760 | bytes 2097152 | tf_op jit(solution)/shard_map/spectral_factors/pallas_call | solution.py:53
  30.6 1.3 %copy-done.1 = f32[4,2,256,256]{3,2,1,0:T(8,128)} copy-done((f32[4,2,256,256]{3,2,1,0:T(8,128)}, f32[4,2,256,256]{3,2,1,0:T(8,128)S(1)}, u32[]{:S(2)}) %copy-start.1) | copy-done | bytes 2097176
  32.0 8.7 %all-to-all-done.1 = f16[16,4,16,256]{3,2,1,0:T(8,128)(2,1)S(1)} async-done(((f16[16,4,16,256]{3,2,1,0:T(8,128)(2,1)}), f16[16,4,16,256]{3,2,1,0:T(8,128)(2,1)S(1)}, u32[]{:S(2)}, u32[]{:S(2)}) %all-to-all-start.1) | async-done | bytes 524320 | tf_op jit(solution)/shard_map/all_to_all | solution.py:172
  40.7 0.1 slice.30
  40.7 0.0 copy-start.5
  40.7 0.1 copy.20
  40.8 0.1 collective-permute-start
  40.9 0.1 convert_multiply_fusion
  41.0 0.1 bitcast_convert_fusion.refs_6_
  41.1 1.3 %collective-permute-done = f16[2,256,256]{2,1,0:T(8,128)(2,1)S(1)} collective-permute-done((f16[2,256,256]{2,1,0:T(8,128)(2,1)S(1)}, f16[2,256,256]{2,1,0:T(8,128)(2,1)S(1)}, u32[]{:S(2)}, u32[]{:S(2)}) %collective-permute-start) | collective-permute-done | bytes 262176 | tf_op jit(solution)/shard_map/ppermute | solution.py:139
  42.5 13.3 %depth_steps.1 = (f32[4,256,256]{2,1,0:T(8,128)S(1)}, f32[2,256,256]{2,1,0:T(8,128)}) custom-call(f32[1]{0:T(128)S(6)} %div.9.refs_0_, s32[1]{0:T(128)} %bitcast.refs_1_, bf16[256,768]{1,0:T(8,128)(2,1)S(1)} %copy-done.5, bf16[768,256]{1,0:T(8,128)(2,1)S(1)} %copy-done.6, f32[4,2,256,256]{3,2,1,0:T(8,128)S(1)} %copy-done.2, f32[2,256,256]{2,1,0:T(8,128)S(1)} %bitcast.43, ...), custom_call_target="tpu_custom_call" | custom-call | flops 8053063680 | bytes 4194304 | tf_op jit(solution)/shard_map/depth_steps/pallas_call | solution.py:123
  55.8 0.1 constant_dynamic-slice_fusion.1
  55.9 0.2 collective-permute-start.1
  56.1 1.8 %collective-permute-done.1 = f32[4,8,16,256]{3,2,0,1:T(8,128)S(1)} collective-permute-done((f32[4,8,16,256]{3,2,0,1:T(8,128)S(1)}, f32[4,8,16,256]{3,2,0,1:T(8,128)S(1)}, u32[]{:S(2)}, u32[]{:S(2)}) %collective-permute-start.1) | collective-permute-done | bytes 524320 | tf_op jit(solution)/shard_map/ppermute | solution.py:139
  57.9 0.1 fusion.11
  58.0 18.7 %all_to_all.15 = f32[8,4,16,256]{3,2,1,0:T(8,128)S(1)} all-to-all(f32[8,4,16,256]{3,2,1,0:T(8,128)S(1)} %fusion.11), channel_id=1, replica_groups={{0,2,4,6,8,10,12,14},{1,3,5,7,9,11,13,15},{16,18,20,22,24,26,28,30},{17..., dimensions={0} | all-to-all | bytes 1048576 | tf_op jit(solution)/shard_map/all_to_all | solution.py:198
  76.7 0.7 reduce_sum.9
  (18 shorter events, 0.2 us)
Async XLA Ops:
  0.6 17.2 %copy-start = (bf16[16,256,256]{2,1,0:T(8,128)(2,1)S(1)}, bf16[16,256,256]{2,1,0:T(8,128)(2,1)}, u32[]{:S(2)}) copy-start(bf16[16,256,256]{2,1,0:T(8,128)(2,1)} %param.9) | copy-start | bytes 6291460
  0.6 18.0 %all-to-all-start = ((bf16[16,16,256]{2,1,0:T(8,128)(2,1)}), bf16[16,16,256]{2,1,0:T(8,128)(2,1)S(1)}, u32[]{:S(2)}, u32[]{:S(2)}) async-start(bf16[16,16,256]{2,1,0:T(8,128)(2,1)} %bitcast.48), calls=%async_computation | async-start | bytes 262144 | tf_op jit(solution)/shard_map/all_to_all | solution.py:151
  18.6 8.8 %copy-start.7 = (f32[2,10,4]{1,2,0:T(4,128)S(1)}, f32[2,10,4]{1,2,0:T(4,128)}, u32[]{:S(2)}) copy-start(f32[2,10,4]{1,2,0:T(4,128)} %param.11) | copy-start | bytes 964
  18.6 8.9 %copy-start.3 = (f32[256,1]{1,0:T(8,128)S(1)}, f32[256,1]{1,0:T(8,128)}, u32[]{:S(2)}) copy-start(f32[256,1]{1,0:T(8,128)} %constant.79.clone.left_ref) | copy-start | bytes 3076
  18.7 8.9 %copy-start.4 = (f32[1,256]{1,0:T(1,128)S(1)}, f32[1,256]{1,0:T(1,128)}, u32[]{:S(2)}) copy-start(f32[1,256]{1,0:T(1,128)} %constant.80.clone.right_ref) | copy-start | bytes 3076
  20.2 20.5 %all-to-all-start.1 = ((f16[16,4,16,256]{3,2,1,0:T(8,128)(2,1)}), f16[16,4,16,256]{3,2,1,0:T(8,128)(2,1)S(1)}, u32[]{:S(2)}, u32[]{:S(2)}) async-start(f16[16,4,16,256]{3,2,1,0:T(8,128)(2,1)} %copy.18), calls=%async_computation.1 | async-start | bytes 1048576 | tf_op jit(solution)/shard_map/all_to_all | solution.py:172
  30.6 1.3 %copy-start.1 = (f32[4,2,256,256]{3,2,1,0:T(8,128)}, f32[4,2,256,256]{3,2,1,0:T(8,128)S(1)}, u32[]{:S(2)}) copy-start(f32[4,2,256,256]{3,2,1,0:T(8,128)S(1)} %spectral_factors.1.refs_4_) | copy-start | bytes 6291460
  40.7 1.7 %copy-start.2 = (f32[4,2,256,256]{3,2,1,0:T(8,128)S(1)}, f32[4,2,256,256]{3,2,1,0:T(8,128)}, u32[]{:S(2)}) copy-start(f32[4,2,256,256]{3,2,1,0:T(8,128)} %copy-done.1) | copy-start | bytes 6291460
  40.7 1.7 %copy-start.5 = (bf16[256,768]{1,0:T(8,128)(2,1)S(1)}, bf16[256,768]{1,0:T(8,128)(2,1)}, u32[]{:S(2)}) copy-start(bf16[256,768]{1,0:T(8,128)(2,1)} %constant.81.clone.refs_2_) | copy-start | bytes 1179652
  40.7 1.7 %copy-start.6 = (bf16[768,256]{1,0:T(8,128)(2,1)S(1)}, bf16[768,256]{1,0:T(8,128)(2,1)}, u32[]{:S(2)}) copy-start(bf16[768,256]{1,0:T(8,128)(2,1)} %constant.82.clone.refs_3_) | copy-start | bytes 1179652
  40.8 1.6 %collective-permute-start = (f16[2,256,256]{2,1,0:T(8,128)(2,1)S(1)}, f16[2,256,256]{2,1,0:T(8,128)(2,1)S(1)}, u32[]{:S(2)}, u32[]{:S(2)}) collective-permute-start(f16[2,256,256]{2,1,0:T(8,128)(2,1)S(1)} %bitcast.46), channel_id=1, source_target_pairs={{0,1},{1,0},{2,3},{3,2},{4,5},{5,4},{6,7},{7,6},{8,9},{9,8},{10,11... | collective-permute-start | bytes 786440 | tf_op jit(solution)/shard_map/ppermute | solution.py:139
  55.9 2.0 %collective-permute-start.1 = (f32[4,8,16,256]{3,2,0,1:T(8,128)S(1)}, f32[4,8,16,256]{3,2,0,1:T(8,128)S(1)}, u32[]{:S(2)}, u32[]{:S(2)}) collective-permute-start(f32[4,8,16,256]{3,2,0,1:T(8,128)S(1)} %bitcast.47), channel_id=1, source_target_pairs={{0,1},{1,0},{2,3},{3,2},{4,5},{5,4},{6,7},{7,6},{8,9},{9,8},{10,11... | collective-permute-start | bytes 1572872 | tf_op jit(solution)/shard_map/ppermute | solution.py:139
where the time goes:
time: 77.9 us; the launch traced here: 77.4 us
  blocking collectives  18.7 us (24%)
  Pallas kernels  16.3 us (21%)
  starting transfers between devices  13.8 us (18%)
  waiting for transfers between devices  11.8 us (15%)
  between operations  8.98 us (12%)
  local copies, waits for them, and re-layouts  5.07 us (7%)
  other arithmetic  1.86 us (2%)
    all_to_all x1, blocking collectives, on_device(): lax.all_to_all(pair_sum.transpose(1, 0, 2, 3), 'freq', split_axis=0, conc...  18.7 us
    pallas_call x1, Pallas kernels, depth_steps(): pl.pallas_call(kernel, out_shape=(jax.ShapeDtypeStruct((depth_count, nx,...  13.3 us
    all_to_all x1, waiting for transfers between devices, on_device(): lax.all_to_all(jnp.concatenate([spectra, halves], axis=1), 'freq', split_...  8.7 us
    all_to_all x1, starting transfers between devices, on_device(): lax.all_to_all(velocity.reshape(devices, local_x, ny), 'freq', split_axis...  7.53 us
    all_to_all x1, starting transfers between devices, on_device(): lax.all_to_all(jnp.concatenate([spectra, halves], axis=1), 'freq', split_...  6.01 us
    ppermute x2, waiting for transfers between devices, swap_cores(): return lax.ppermute(array, 'freq', [(i, i ^ 1) for i in range(count)])  3.12 us
    pallas_call x1, Pallas kernels, spectral_factors(): pl.pallas_call(factors_kernel, out_shape=jax.ShapeDtypeStruct((poly_coef....  3.07 us
  transfers between devices with their start and end apart: 4, of which 3 were waited for; matrix products, arithmetic and copies ran while one was open for 5% of the time, Pallas kernels for 4%

commit v1 on v0

v1 whole, which is shorter than its diff:
```python
import math

import jax
import jax.numpy as jnp
import numpy as np
from jax import lax
from jax.experimental import pallas as pl
from jax.experimental.pallas import tpu as pltpu
from jax.sharding import PartitionSpec as P

SPECTRA_SCALE = 512.0


def sine_transform(size):
    index = np.arange(1, size + 1)
    matrix = np.sqrt(2.0 / (size + 1)) * np.sin(np.pi * np.outer(index, index) / (size + 1))
    return matrix, 2.0 + 2.0 * np.cos(np.pi * index / (size + 1))

def halves_of(matrix):
    high = matrix.astype(jnp.bfloat16)
    return high, (matrix - high.astype(np.float64)).astype(jnp.bfloat16)

def split(values):
    high = values.astype(jnp.bfloat16)
    return high, (values - high.astype(jnp.float32)).astype(jnp.bfloat16)

def dot(a, b):
    return jnp.dot(a, b, preferred_element_type=jnp.float32)

def factors_kernel(coef_ref, left_ref, right_ref, out_ref):
    term_count, power_count = coef_ref.shape[1:]
    block = 32
    def rows_step(i, carry):
        rows = pl.ds(pl.multiple_of(i * block, block), block)
        g = left_ref[rows, :] * right_ref[0:1, :] * 0.125 - 1.0
        twice = 2.0 * g
        sums = [[coef_ref[c, 0, j] + coef_ref[c, 1, j] * g for c in range(2)] for j in range(power_count)]
        before, now = jnp.ones_like(g), g
        for k in range(2, term_count):
            before, now = now, twice * now - before
            for j in range(power_count):
                for c in range(2):
                    sums[j][c] = sums[j][c] + coef_ref[c, k, j] * now
        for j in range(power_count):
            for c in range(2):
                out_ref[j, c, rows, :] = sums[j][c]
        return carry
    lax.fori_loop(0, left_ref.shape[0] // block, rows_step, 0)

def spectral_factors(poly_coef, nx, ny):
    _, lx = sine_transform(nx)
    _, ly = sine_transform(ny)
    left = jnp.asarray(np.broadcast_to(lx[:, None], (nx, 1)), jnp.float32)
    right = jnp.asarray(ly[None, :], jnp.float32)
    vmem = pl.BlockSpec(memory_space=pltpu.VMEM)
    return pl.pallas_call(
        factors_kernel,
        out_shape=pltpu.HBM((poly_coef.shape[2], 2, nx, ny), jnp.float32),
        in_specs=[pl.BlockSpec(memory_space=pltpu.SMEM), vmem, vmem],
        out_specs=vmem,
        compiler_params=pltpu.CompilerParams(vmem_limit_bytes=6 * 1024 * 1024),
        cost_estimate=pl.CostEstimate(
            flops=poly_coef.size * 2 * nx * ny, bytes_accessed=32 * nx * ny, transcendentals=0
        ),
        name="spectral_factors",
    )(poly_coef, left, right)

def right_product(values, matrix_ref):
    high, low = split(values)
    return dot(high, matrix_ref[0]) + dot(low, matrix_ref[0]) + dot(high, matrix_ref[1])


def left_product(matrix_ref, values):
    high, low = split(values)
    return dot(matrix_ref[0], high) + dot(matrix_ref[0], low) + dot(matrix_ref[1], high)


def step_part(left_ref, right_ref, factor_ref, spectrum, j, c):
    if c == 0:
        mixed = factor_ref[j, 0] * spectrum[0] - factor_ref[j, 1] * spectrum[1]
    else:
        mixed = factor_ref[j, 0] * spectrum[1] + factor_ref[j, 1] * spectrum[0]
    return right_product(left_product(left_ref, mixed), right_ref)


def first_kernel(left_ref, right_ref, factor_hbm, start_ref, part_ref, spectrum, factor_ref, sem):
    fetch = pltpu.make_async_copy(factor_hbm, factor_ref, sem)
    fetch.start()
    for c in range(2):
        spectrum[c] = left_product(left_ref, right_product(start_ref[c], right_ref))
    fetch.wait()
    for j in range(part_ref.shape[0]):
        for c in range(2):
            part_ref[j, c] = step_part(left_ref, right_ref, factor_ref, spectrum, j, c)


def depth_kernel(
    slot_ref, place_ref, left_ref, right_ref, factor_hbm, part_ref, mine_ref, other_ref,
    keep_ref, send_ref, field_ref, state, spectrum, slow, factor_ref, sems, *, total_freq,
):
    chips, depth_count, local_x, _ = mine_ref.shape
    power_count = factor_ref.shape[0]
    image_scale = 1.0 / math.sqrt(total_freq)
    scale = (slot_ref[place_ref[0]] + 1).astype(jnp.float32) / total_freq
    core = lax.rem(place_ref[0], 2)

    def rows_of(chip, number):
        first = (2 * chip + number) * local_x
        return slice(first, first + local_x)

    def load_slow(z):
        for number in range(2):
            @pl.when(core == number)
            def _():
                for chip in range(chips):
                    slow[rows_of(chip, number), :] = scale / mine_ref[chip, z].astype(jnp.float32)
                    slow[rows_of(chip, 1 - number), :] = scale / other_ref[chip, z].astype(jnp.float32)

    def store_image(z):
        for number in range(2):
            @pl.when(core == number)
            def _():
                for chip in range(chips):
                    keep_ref[chip, z] = state[0, rows_of(chip, number), :] * image_scale
                    send_ref[chip, z] = state[0, rows_of(chip, 1 - number), :] * image_scale

    fetches = [
        pltpu.make_async_copy(factor_hbm.at[j], factor_ref.at[j], sems.at[j]) for j in range(power_count)
    ]
    for fetch in fetches:
        fetch.start()
    load_slow(0)
    for c in range(2):
        total = part_ref[power_count - 1, c]
        for j in range(power_count - 2, -1, -1):
            total = total * slow[...] + part_ref[j, c]
        state[c] = total
    store_image(0)

    def depth_step(z, carry):
        load_slow(z)
        for c in range(2):
            spectrum[c] = left_product(left_ref, right_product(state[c], right_ref))

        @pl.when(z == 1)
        def _():
            for fetch in fetches:
                fetch.wait()

        for c in range(2):
            state[c] = step_part(left_ref, right_ref, factor_ref, spectrum, power_count - 1, c)
            for j in range(power_count - 2, -1, -1):
                state[c] = state[c] * slow[...] + step_part(left_ref, right_ref, factor_ref, spectrum, j, c)
        store_image(z)
        return carry

    lax.fori_loop(1, depth_count, depth_step, 0)
    field_ref[...] = state[...]
    peak = jnp.max(jnp.abs(keep_ref[:, :depth_count]), axis=(0, 1))
    peak = jnp.maximum(peak, jnp.max(jnp.abs(send_ref[:, :depth_count]), axis=(0, 1)))
    peak = jnp.max(jnp.max(peak, axis=0, keepdims=True), axis=1, keepdims=True)
    for chip in range(chips):
        keep_ref[chip, depth_count] = jnp.broadcast_to(peak, keep_ref.shape[2:])
        send_ref[chip, depth_count] = jnp.broadcast_to(peak, keep_ref.shape[2:])


def transform(size):
    return jnp.asarray(np.stack(halves_of(sine_transform(size)[0])))


SMEM = pl.BlockSpec(memory_space=pltpu.SMEM)
VMEM = pl.BlockSpec(memory_space=pltpu.VMEM)
HBM = pl.BlockSpec(memory_space=pltpu.HBM)


def in_vmem(array):
    return pltpu.with_memory_space_constraint(array, pltpu.VMEM)


def in_hbm(array):
    return pltpu.with_memory_space_constraint(array, pltpu.HBM)


def first_parts(left, right, factors, start):
    power_count, _, nx, ny = factors.shape
    return pl.pallas_call(
        first_kernel,
        out_shape=pltpu.VMEM((power_count, 2, nx, ny), jnp.float32),
        in_specs=[VMEM, VMEM, HBM, VMEM],
        out_specs=VMEM,
        scratch_shapes=[
            pltpu.VMEM((2, nx, ny), jnp.float32),
            pltpu.VMEM(factors.shape, jnp.float32),
            pltpu.SemaphoreType.DMA,
        ],
        compiler_params=pltpu.CompilerParams(vmem_limit_bytes=8 * 1024 * 1024),
        cost_estimate=pl.CostEstimate(
            flops=120 * nx * ny * (nx + ny) // 2, bytes_accessed=64 * nx * ny, transcendentals=0
        ),
        name="first_parts",
    )(left, right, in_hbm(factors), start)


def depth_steps(freq_slot, place, left, right, factors, parts, mine, other):
    chips, depth_count, local_x, ny = mine.shape
    _, _, nx, _ = factors.shape

    def kernel(*refs):
        depth_kernel(*refs, total_freq=freq_slot.shape[0])

    share = jax.ShapeDtypeStruct((chips, depth_count + 1, local_x, ny), jnp.float32)
    return pl.pallas_call(
        kernel,
        out_shape=(share, share, jax.ShapeDtypeStruct((2, nx, ny), jnp.float32)),
        in_specs=[SMEM, SMEM, VMEM, VMEM, HBM, VMEM, VMEM, VMEM],
        out_specs=(VMEM, VMEM, VMEM),
        scratch_shapes=[
            pltpu.VMEM((2, nx, ny), jnp.float32),
            pltpu.VMEM((2, nx, ny), jnp.float32),
            pltpu.VMEM((nx, ny), jnp.float32),
            pltpu.VMEM(factors.shape, jnp.float32),
            pltpu.SemaphoreType.DMA((factors.shape[0],)),
        ],
        compiler_params=pltpu.CompilerParams(vmem_limit_bytes=10 * 1024 * 1024),
        cost_estimate=pl.CostEstimate(
            flops=depth_count * 120 * nx * ny * (nx + ny) // 2, bytes_accessed=64 * nx * ny, transcendentals=0
        ),
        name="depth_steps",
    )(freq_slot, place, left, right, in_hbm(factors), in_vmem(parts), mine, other)


def spectra_kernel(
    slot_hbm, table_hbm, traces_hbm, speed_hbm, out_ref, slot_ref, table_ref, traces_ref, speed_ref, bins, sems
):
    slots, _, local_x, ny = out_ref.shape
    chunk = max(local_x // 4, 1)
    copies = [
        pltpu.make_async_copy(table_hbm, table_ref, sems.at[0]),
        pltpu.make_async_copy(slot_hbm, slot_ref, sems.at[1]),
        pltpu.make_async_copy(speed_hbm, speed_ref, sems.at[2]),
    ]
    for i, x in enumerate(range(0, local_x, chunk)):
        part = pl.ds(x, chunk)
        copies.append(pltpu.make_async_copy(traces_hbm.at[part], traces_ref.at[part], sems.at[3 + i]))
    for copy in copies:
        copy.start()
    copies[0].wait()
    for i, x in enumerate(range(0, local_x, chunk)):
        copies[3 + i].wait()
        rows = traces_ref[x : x + chunk].reshape(chunk * ny, traces_ref.shape[2])
        result = lax.dot_general(
            table_ref[...], rows, (((1,), (1,)), ((), ())), preferred_element_type=jnp.float32
        )
        for k in range(chunk):
            bins[:, x + k, :] = result[:, k * ny : (k + 1) * ny]
    copies[1].wait()
    copies[2].wait()
    for f in range(slots):
        for c in range(2):
            out_ref[f, c] = bins[2 * slot_ref[f] + c] * SPECTRA_SCALE
        out_ref[f, 2] = speed_ref[f].astype(jnp.float32)


def position_spectra(freq_slot, traces, speed):
    local_x, ny, sample_count = traces.shape
    slots = freq_slot.shape[0]
    index = np.arange(1, slots + 1)[:, None] * np.arange(sample_count)[None, :] % sample_count
    phases = index.astype(np.float32) * np.float32(2.0 * math.pi / sample_count)
    table = np.stack([np.cos(phases), -np.sin(phases)], axis=1) / np.float32(math.sqrt(sample_count))
    table = jnp.asarray(table.reshape(2 * slots, sample_count).astype(jnp.bfloat16))
    return pl.pallas_call(
        spectra_kernel,
        out_shape=jax.ShapeDtypeStruct((slots, 3, local_x, ny), jnp.float32),
        in_specs=[HBM] * 4,
        out_specs=VMEM,
        scratch_shapes=[
            pltpu.SMEM((slots,), jnp.int32),
            pltpu.VMEM((2 * slots, sample_count), jnp.bfloat16),
            pltpu.VMEM(traces.shape, jnp.bfloat16),
            pltpu.VMEM(speed.shape, jnp.bfloat16),
            pltpu.VMEM((2 * slots, local_x, ny), jnp.float32),
            pltpu.SemaphoreType.DMA((7,)),
        ],
        compiler_params=pltpu.CompilerParams(vmem_limit_bytes=8 * 1024 * 1024),
        cost_estimate=pl.CostEstimate(
            flops=4 * slots * traces.size, bytes_accessed=2 * traces.size, transcendentals=0
        ),
        name="position_spectra",
    )(in_hbm(freq_slot), in_hbm(table), in_hbm(traces), in_hbm(speed))


def swap_cores(array, count):
    return lax.ppermute(array, "freq", [(i, i ^ 1) for i in range(count)])


def on_device(traces, velocity, poly_coef, freq_slot, depth_owner):
    devices = lax.axis_size("freq")
    local_x, ny, _ = traces.shape
    nx = devices * local_x
    chips = devices // 2
    depth_count = depth_owner.shape[0]
    place = lax.axis_index("freq").astype(jnp.int32).reshape(1)
    same_core = [[i for i in range(devices) if i % 2 == c] for c in range(2)]

    spectra = position_spectra(freq_slot, traces, velocity.reshape(devices, local_x, ny))
    received = lax.all_to_all(
        spectra.astype(jnp.float16), "freq", split_axis=0, concat_axis=0, tiled=True
    )
    received, factors = lax.optimization_barrier((received, spectral_factors(poly_coef, nx, ny)))
    start = received[:, :2].transpose(1, 0, 2, 3).reshape(2, nx, ny).astype(jnp.float32) / SPECTRA_SCALE

    owned = (depth_owner[:, None] == jnp.arange(devices, dtype=jnp.int32)[None, :]).astype(jnp.bfloat16)
    by_rows = received[:, 2].astype(jnp.bfloat16).reshape(devices, local_x * ny)
    chosen = jnp.dot(owned, by_rows, preferred_element_type=jnp.float32).astype(jnp.bfloat16)
    chosen = jnp.broadcast_to(
        chosen.reshape(1, depth_count, local_x, ny), (chips, depth_count, local_x, ny)
    )
    mine = lax.all_to_all(
        chosen, "freq", split_axis=0, concat_axis=0, tiled=True, axis_index_groups=same_core
    )
    left, right = transform(nx), transform(ny)
    parts, mine = lax.optimization_barrier((first_parts(left, right, factors, start), mine))
    other = swap_cores(mine, devices)
    keep, send, wavefield = depth_steps(
        freq_slot,
        place,
        left,
        right,
        factors,
        parts,
        mine,
        other,
    )

    total = keep + swap_cores(send, devices)
    power = jnp.ceil(jnp.log2(jnp.maximum(total[:, depth_count:], 1e-30)))
    packed = jnp.concatenate([total[:, :depth_count] * jnp.exp2(-power), power], axis=1)
    shares = lax.all_to_all(
        packed.astype(jnp.float16),
        "freq",
        split_axis=0,
        concat_axis=0,
        tiled=True,
        axis_index_groups=same_core,
    ).astype(jnp.float32)
    image = jnp.sum(shares[:, :depth_count] * jnp.exp2(shares[:, depth_count:]), axis=0)
    return (image, wavefield[:, None])


def solution(mesh):
    return jax.shard_map(
        on_device,
        mesh=mesh,
        in_specs=(
            P(("group", "freq"), None, None),
            P(("group", "freq"), None, None),
            P(),
            P(),
            P("group"),
        ),
        out_specs=(P(None, ("group", "freq"), None), P(None, ("group", "freq"), None, None)),
        check_vma=False,
    )
```

time: 77.9 us -> 69 us (0.89)
  between operations: 8.98 us -> 0.8 us
  Pallas kernels: 16.3 us -> 22.3 us
  waiting for transfers between devices: 11.8 us -> 16.6 us
  local copies, waits for them, and re-layouts: 5.07 us -> 0.95 us
  blocking collectives: 18.7 us -> 14.6 us
  starting transfers between devices: 13.8 us -> 11 us
    pallas_call x2 -> x4, Pallas kernels: 16.3 us -> 22.3 us  [the longest x1 11.7 us: depth_steps(): pl.pallas_call(kernel, out_shape=(share, share, jax.ShapeDtypeStruct((2,...]
    all_to_all x2, waiting for transfers between devices: 8.7 us -> 13.1 us  [the longest x1 7.68 us: on_device(): lax.all_to_all(spectra.astype(jnp.float16), 'freq', split_axis=0, concat_...]
    all_to_all x1, blocking collectives: 18.7 us -> 14.6 us  [on_device(): lax.all_to_all(packed.astype(jnp.float16), 'freq', split_axis=0, concat_a...]
    all_to_all x2, starting transfers between devices: 13.5 us -> 10.8 us  [the longest x1 7.38 us: on_device(): lax.all_to_all(spectra.astype(jnp.float16), 'freq', split_axis=0, concat_...]
    slice x3 -> x0, local copies, waits for them, and re-layouts: 1.52 us -> none  [the longest x1 1.42 us: on_device(): depth_owner[z]]
    unnamed x17 -> x15, local copies, waits for them, and re-layouts: 1.47 us -> 0.19 us
    concatenate x1 -> x0, local copies, waits for them, and re-layouts: 1 us -> none  [on_device(): jnp.concatenate([spectra, halves], axis=1)]
    convert_element_type x3, other arithmetic: 0.1 us -> 0.91 us  [the longest x1 0.82 us: on_device(): spectra.astype(jnp.float16)]
  transfers between devices with their start and end apart: 4 -> 4, of which waited for: 3 -> 4; matrix products, arithmetic and copies ran while one was open for 5% -> 0% of each run, Pallas kernels for 4% -> 12%
where the time goes in v1:
time: 69 us; the launch traced here: 68.5 us
  Pallas kernels  22.3 us (32%)
  waiting for transfers between devices  16.6 us (24%)
  blocking collectives  14.6 us (21%)
  starting transfers between devices  11 us (16%)
  other arithmetic  2 us (3%)
  local copies, waits for them, and re-layouts  0.95 us (1%)
  between operations  0.8 us (1%)
    all_to_all x1, blocking collectives, on_device(): lax.all_to_all(packed.astype(jnp.float16), 'freq', split_axis=0, concat_a...  14.6 us
    pallas_call x1, Pallas kernels, depth_steps(): pl.pallas_call(kernel, out_shape=(share, share, jax.ShapeDtypeStruct((2,...  11.7 us
    all_to_all x1, waiting for transfers between devices, on_device(): lax.all_to_all(spectra.astype(jnp.float16), 'freq', split_axis=0, concat_...  7.68 us
    all_to_all x1, starting transfers between devices, on_device(): lax.all_to_all(spectra.astype(jnp.float16), 'freq', split_axis=0, concat_...  7.38 us
    all_to_all x1, waiting for transfers between devices, on_device(): lax.all_to_all(chosen, 'freq', split_axis=0, concat_axis=0, tiled=True, a...  5.46 us
    pallas_call x1, Pallas kernels, spectral_factors(): pl.pallas_call(factors_kernel, out_shape=pltpu.HBM((poly_coef.shape[2], 2...  4.4 us
    pallas_call x1, Pallas kernels, first_parts(): pl.pallas_call(first_kernel, out_shape=pltpu.VMEM((power_count, 2, nx, ny...  3.81 us
    ppermute x2, waiting for transfers between devices, swap_cores(): return lax.ppermute(array, 'freq', [(i, i ^ 1) for i in range(count)])  3.47 us
  transfers between devices with their start and end apart: 4, of which 4 were waited for; matrix products, arithmetic and copies ran while one was open for 0% of the time, Pallas kernels for 12%

profile of v1, /device:TPU:0, one launch (start us, length us, event | category | flops | bytes accessed | tf_op | source)
XLA Modules:
  0.0 68.5 jit_solution(10068605500080020960)
XLA Ops:
  0.6 0.0 copy-start.4
  0.6 0.0 copy-start
  0.7 0.0 copy-start.1
  0.7 2.4 %position_spectra.1 = f32[16,3,16,256]{3,2,1,0:T(8,128)S(1)} custom-call(s32[16]{0:T(128)} %refs_0_.1, bf16[32,256]{1,0:T(8,128)(2,1)} %constant.23.clone.table_hbm, bf16[16,256,256]{2,1,0:T(8,128)(2,1)} %traces_hbm.1, bf16[16,16,256]{2,1,0:T(8,128)(2,1)} %bitcast.23), custom_call_target="tpu_custom_call" | custom-call | flops 67108864 | bytes 2097152 | tf_op jit(solution)/shard_map/position_spectra/pallas_call | solution.py:271
  3.1 0.0 copy-start.5
  3.1 0.8 %convert_element_type.23 = f16[16,3,16,256]{3,2,1,0:T(8,128)(2,1)} convert(f32[16,3,16,256]{3,2,1,0:T(8,128)S(1)} %position_spectra.1) | non-fusion elementwise | flops 196608 | bytes 1179648 | tf_op jit(solution)/shard_map/convert_element_type | solution.py:307
  3.9 7.4 %all-to-all-start = ((f16[16,3,16,256]{3,2,1,0:T(8,128)(2,1)}), f16[16,3,16,256]{3,2,1,0:T(8,128)(2,1)S(1)}, u32[]{:S(2)}, u32[]{:S(2)}) async-start(f16[16,3,16,256]{3,2,1,0:T(8,128)(2,1)} %convert_element_type.23), calls=%async_computation | async-start | bytes 786432 | tf_op jit(solution)/shard_map/all_to_all | solution.py:306
  11.3 0.0 copy-done.4
  11.3 0.1 copy.12.coef_ref
  11.4 0.0 copy-done
  11.4 0.0 copy-done.1
  11.4 4.4 %spectral_factors.1.factor_hbm.refs_4_ = f32[4,2,256,256]{3,2,1,0:T(8,128)} custom-call(f32[2,10,4]{2,1,0:T(8,128)S(1)} %copy.12.coef_ref, f32[256,1]{1,0:T(8,128)S(1)} %copy-done, f32[1,256]{1,0:T(1,128)S(1)} %copy-done.1), custom_call_target="tpu_custom_call" | custom-call | flops 10485760 | bytes 2097152 | tf_op jit(solution)/shard_map/spectral_factors/pallas_call | solution.py:56
  15.8 7.7 %all-to-all-done = f16[16,3,16,256]{3,2,1,0:T(8,128)(2,1)S(1)} async-done(((f16[16,3,16,256]{3,2,1,0:T(8,128)(2,1)}), f16[16,3,16,256]{3,2,1,0:T(8,128)(2,1)S(1)}, u32[]{:S(2)}, u32[]{:S(2)}) %all-to-all-start) | async-done | bytes 393248 | tf_op jit(solution)/shard_map/all_to_all | solution.py:306
  23.6 0.2 convolution_convert_fusion
  23.8 0.7 %broadcast_in_dim.13 = bf16[8,4,16,256]{3,2,1,0:T(8,128)(2,1)} broadcast(bf16[4,16,256]{2,1,0:T(8,128)(2,1)S(1)} %bitcast.25), dimensions={1,2,3} | broadcast | bytes 294912 | tf_op jit(solution)/shard_map/broadcast_in_dim | solution.py:315
  24.6 3.4 %all-to-all-start.1 = ((bf16[8,4,16,256]{3,2,1,0:T(8,128)(2,1)}), bf16[8,4,16,256]{3,2,1,0:T(8,128)(2,1)S(1)}, u32[]{:S(2)}, u32[]{:S(2)}) async-start(bf16[8,4,16,256]{3,2,1,0:T(8,128)(2,1)} %broadcast_in_dim.13), calls=%async_computation.1 | async-start | bytes 524288 | tf_op jit(solution)/shard_map/all_to_all | solution.py:318
  28.0 0.1 multiply_bitcast_fusion
  28.1 0.0 copy-start.2
  28.1 3.8 %first_parts.1.refs_5_ = f32[4,2,256,256]{3,2,1,0:T(8,128)S(1)} custom-call(bf16[2,256,256]{2,1,0:T(8,128)(2,1)S(1)} %copy-done.3, bf16[2,256,256]{2,1,0:T(8,128)(2,1)S(1)} %copy-done.3, f32[4,2,256,256]{3,2,1,0:T(8,128)} %spectral_factors.1.factor_hbm.refs_4_, f32[2,256,256]{2,1,0:T(8,128)S(1)} %bitcast.20), custom_call_target="tpu_custom_call" | custom-call | flops 2013265920 | bytes 4194304 | tf_op jit(solution)/shard_map/first_parts/pallas_call | solution.py:186
  31.9 5.5 %all-to-all-done.1.refs_6_ = bf16[8,4,16,256]{3,2,1,0:T(8,128)(2,1)S(1)} async-done(((bf16[8,4,16,256]{3,2,1,0:T(8,128)(2,1)}), bf16[8,4,16,256]{3,2,1,0:T(8,128)(2,1)S(1)}, u32[]{:S(2)}, u32[]{:S(2)}) %all-to-all-start.1) | async-done | bytes 262176 | tf_op jit(solution)/shard_map/all_to_all | solution.py:318
  37.4 0.0 collective-permute-start
  37.4 1.5 %collective-permute-done.refs_7_ = bf16[8,4,16,256]{3,2,1,0:T(8,128)(2,1)S(1)} collective-permute-done((bf16[8,4,16,256]{3,2,1,0:T(8,128)(2,1)S(1)}, bf16[8,4,16,256]{3,2,1,0:T(8,128)(2,1)S(1)}, u32[]{:S(2)}, u32[]{:S(2)}) %collective-permute-start) | collective-permute-done | bytes 262176 | tf_op jit(solution)/shard_map/ppermute | solution.py:293
  38.9 11.7 %depth_steps.1 = (f32[8,5,16,256]{3,2,1,0:T(8,128)S(1)}, f32[8,5,16,256]{3,2,1,0:T(8,128)S(1)}, f32[2,256,256]{2,1,0:T(8,128)}) custom-call(s32[16]{0:T(128)S(1)} %copy-done.2, s32[1]{0:T(128)} %bitcast.refs_1_, bf16[2,256,256]{2,1,0:T(8,128)(2,1)S(1)} %copy-done.3, bf16[2,256,256]{2,1,0:T(8,128)(2,1)S(1)} %copy-done.3, ...), custom_call_target="tpu_custom_call" | custom-call | flops 8053063680 | bytes 4194304 | tf_op jit(solution)/shard_map/depth_steps/pallas_call | solution.py:212
  50.7 0.2 collective-permute-start.1
  50.9 1.9 %collective-permute-done.1 = f32[8,5,16,256]{3,2,1,0:T(8,128)S(1)} collective-permute-done((f32[8,5,16,256]{3,2,1,0:T(8,128)S(1)}, f32[8,5,16,256]{3,2,1,0:T(8,128)S(1)}, u32[]{:S(2)}, u32[]{:S(2)}) %collective-permute-start.1) | collective-permute-done | bytes 655392 | tf_op jit(solution)/shard_map/ppermute | solution.py:293
  52.8 0.1 add.3
  52.9 0.1 exponential_bitcast_fusion
  53.0 0.1 fusion.1
  53.1 0.1 pad_maximum_fusion
  53.1 14.6 %all_to_all.15 = f16[8,5,16,256]{3,2,1,0:T(8,128)(2,1)S(1)} all-to-all(f16[8,5,16,256]{3,2,1,0:T(8,128)(2,1)S(1)} %pad_maximum_fusion), channel_id=1, replica_groups={{0,2,4,6,8,10,12,14},{1,3,5,7,9,11,13,15},{16,18,20,22,24,26,28,30},{17..., dimensions={0} | all-to-all | bytes 655360 | tf_op jit(solution)/shard_map/all_to_all | solution.py:338
  67.7 0.1 convert_element_type.28
  67.8 0.7 %fusion = f32[4,16,256]{2,1,0:T(8,128)} fusion(f32[8,5,16,256]{3,2,1,0:T(8,128)S(1)} %convert_element_type.28, f32[8,16,256]{2,1,0:T(8,128)S(1)} %fusion.3), kind=kLoop, calls=%fused_computation.2 | loop fusion | flops 245760 | bytes 720896 | tf_op jit(solution)/shard_map/reduce_sum | solution.py:346
  (9 shorter events, 0.1 us)
Async XLA Ops:
  0.6 10.7 %copy-start.4 = (f32[2,10,4]{1,2,0:T(4,128)S(1)}, f32[2,10,4]{1,2,0:T(4,128)}, u32[]{:S(2)}) copy-start(f32[2,10,4]{1,2,0:T(4,128)} %param.12) | copy-start | bytes 964
  0.6 10.8 %copy-start = (f32[256,1]{1,0:T(8,128)S(1)}, f32[256,1]{1,0:T(8,128)}, u32[]{:S(2)}) copy-start(f32[256,1]{1,0:T(8,128)} %constant.24.clone.left_ref) | copy-start | bytes 3076
  0.7 10.8 %copy-start.1 = (f32[1,256]{1,0:T(1,128)S(1)}, f32[1,256]{1,0:T(1,128)}, u32[]{:S(2)}) copy-start(f32[1,256]{1,0:T(1,128)} %constant.25.clone.right_ref) | copy-start | bytes 3076
  3.1 20.5 %copy-start.5 = (s32[4]{0:T(128)S(1)}, s32[4]{0:T(128)}, u32[]{:S(2)}) copy-start(s32[4]{0:T(128)} %param.14) | copy-start | bytes 52
  3.9 19.6 %all-to-all-start = ((f16[16,3,16,256]{3,2,1,0:T(8,128)(2,1)}), f16[16,3,16,256]{3,2,1,0:T(8,128)(2,1)S(1)}, u32[]{:S(2)}, u32[]{:S(2)}) async-start(f16[16,3,16,256]{3,2,1,0:T(8,128)(2,1)} %convert_element_type.23), calls=%async_computation | async-start | bytes 786432 | tf_op jit(solution)/shard_map/all_to_all | solution.py:306
  15.8 12.2 %copy-start.3 = (bf16[2,256,256]{2,1,0:T(8,128)(2,1)S(1)}, bf16[2,256,256]{2,1,0:T(8,128)(2,1)}, u32[]{:S(2)}) copy-start(bf16[2,256,256]{2,1,0:T(8,128)(2,1)} %constant.26.clone.left_ref.right_ref.refs_2_.refs_3_) | copy-start | bytes 786436
  24.6 12.8 %all-to-all-start.1 = ((bf16[8,4,16,256]{3,2,1,0:T(8,128)(2,1)}), bf16[8,4,16,256]{3,2,1,0:T(8,128)(2,1)S(1)}, u32[]{:S(2)}, u32[]{:S(2)}) async-start(bf16[8,4,16,256]{3,2,1,0:T(8,128)(2,1)} %broadcast_in_dim.13), calls=%async_computation.1 | async-start | bytes 524288 | tf_op jit(solution)/shard_map/all_to_all | solution.py:318
  28.1 10.8 %copy-start.2 = (s32[16]{0:T(128)S(1)}, s32[16]{0:T(128)}, u32[]{:S(2)}) copy-start(s32[16]{0:T(128)} %refs_0_.1) | copy-start | bytes 196
  37.4 1.5 %collective-permute-start = (bf16[8,4,16,256]{3,2,1,0:T(8,128)(2,1)S(1)}, bf16[8,4,16,256]{3,2,1,0:T(8,128)(2,1)S(1)}, u32[]{:S(2)}, u32[]{:S(2)}) collective-permute-start(bf16[8,4,16,256]{3,2,1,0:T(8,128)(2,1)S(1)} %all-to-all-done.1.refs_6_), channel_id=1, source_target_pairs={{0,1},{1,0},{2,3},{3,2},{4,5},{5,4},{6,7},{7,6},{8,9},{9,8},{10,11... | collective-permute-start | bytes 786440 | tf_op jit(solution)/shard_map/ppermute | solution.py:293
  50.7 2.2 %collective-permute-start.1 = (f32[8,5,16,256]{3,2,1,0:T(8,128)S(1)}, f32[8,5,16,256]{3,2,1,0:T(8,128)S(1)}, u32[]{:S(2)}, u32[]{:S(2)}) collective-permute-start(f32[8,5,16,256]{3,2,1,0:T(8,128)S(1)} %get-tuple-element.14), channel_id=1, source_target_pairs={{0,1},{1,0},{2,3},{3,2},{4,5},{5,4},{6,7},{7,6},{8,9},{9,8},{10,11... | collective-permute-start | bytes 1966088 | tf_op jit(solution)/shard_map/ppermute | solution.py:293

commit v2 on v1

v2 whole, which is shorter than its diff:
```python
import math

import jax
import jax.numpy as jnp
import numpy as np
from jax import lax
from jax.experimental import pallas as pl
from jax.experimental.pallas import tpu as pltpu
from jax.sharding import PartitionSpec as P

SPECTRA_SCALE = 512.0
SMEM = pl.BlockSpec(memory_space=pltpu.SMEM)
VMEM = pl.BlockSpec(memory_space=pltpu.VMEM)
HBM = pl.BlockSpec(memory_space=pltpu.HBM)


def in_vmem(array):
    return pltpu.with_memory_space_constraint(array, pltpu.VMEM)


def in_hbm(array):
    return pltpu.with_memory_space_constraint(array, pltpu.HBM)


def eigenvalues(size):
    values = 2.0 + 2.0 * np.cos(np.pi * np.arange(1, size + 1) / (size + 1))
    return np.concatenate([values[0::2], values[1::2]])


def folded_sines(size):
    index = np.arange(1, size + 1)
    matrix = np.sqrt(2.0 / (size + 1)) * np.sin(np.pi * np.outer(index, index) / (size + 1))
    return matrix[: size // 2, 0::2], matrix[: size // 2, 1::2]


def right_matrices(size):
    out = []
    even, odd = folded_sines(size)
    for matrix in (even, odd, even.T, odd.T):
        high = matrix.astype(jnp.bfloat16)
        low = (matrix - high.astype(np.float64)).astype(jnp.bfloat16)
        out.append(np.block([[high, low], [high, np.zeros_like(low)]]))
    return np.stack(out)


def fold_order(size):
    half = size // 2
    return np.concatenate([np.arange(half), np.arange(size - 1, half - 1, -1)])


def fold_matrix(size):
    return np.eye(size)[fold_order(size)].astype(jnp.bfloat16)


def split(values):
    high = values.astype(jnp.bfloat16)
    return high, (values - high.astype(jnp.float32)).astype(jnp.bfloat16)


def dot(a, b):
    return jnp.dot(a, b, preferred_element_type=jnp.float32)


def along_y(values, matrix):
    half = values.shape[1]
    both = dot(jnp.concatenate(split(values), axis=1), matrix)
    return both[:, :half] + both[:, half:]


def along_x(values, matrix):
    half = values.shape[0]
    both = dot(matrix, jnp.concatenate(split(values), axis=0))
    return both[:half] + both[half:]


def forward(values, left_ref, right_ref):
    half = values.shape[1] // 2
    a, b = values[:, :half], values[:, half:]
    values = jnp.concatenate([along_y(a + b, right_ref[0]), along_y(a - b, right_ref[1])], axis=1)
    half = values.shape[0] // 2
    a, b = values[:half], values[half:]
    return jnp.concatenate([along_x(a + b, left_ref[0]), along_x(a - b, left_ref[1])], axis=0)


def inverse_x(values, left_ref):
    half = values.shape[0] // 2
    even, odd = along_x(values[:half], left_ref[2]), along_x(values[half:], left_ref[3])
    return jnp.concatenate([even + odd, even - odd], axis=0)


def inverse_y(values, right_ref):
    half = values.shape[1] // 2
    even, odd = along_y(values[:, :half], right_ref[2]), along_y(values[:, half:], right_ref[3])
    return jnp.concatenate([even + odd, even - odd], axis=1)


def reorder(values, left, right):
    high, low = split(values)
    values = dot(high, right) + dot(low, right)
    high, low = split(values)
    return dot(left, high) + dot(left, low)


def half_parts(left_ref, factor_ref, spectrum, columns, parts):
    for j in range(factor_ref.shape[0]):
        for c in parts:
            if c == 0:
                mixed = factor_ref[j, 0] * spectrum[0] - factor_ref[j, 1] * spectrum[1]
            else:
                mixed = factor_ref[j, 0] * spectrum[1] + factor_ref[j, 1] * spectrum[0]
            columns[j, c] = inverse_x(mixed, left_ref)


def sum_powers(right_ref, columns, slow, state, parts):
    power_count = columns.shape[0]
    for j in range(power_count - 1, -1, -1):
        for c in parts:
            part = inverse_y(columns[j, c], right_ref)
            state[c] = part if j == power_count - 1 else state[c] * slow[...] + part


def factors_kernel(coef_ref, left_ref, right_ref, out_ref):
    term_count, power_count = coef_ref.shape[1:]
    block = 32

    def rows_step(i, carry):
        rows = pl.ds(pl.multiple_of(i * block, block), block)
        g = left_ref[rows, :] * right_ref[0:1, :] * 0.125 - 1.0
        twice = 2.0 * g
        sums = [[coef_ref[c, 0, j] + coef_ref[c, 1, j] * g for c in range(2)] for j in range(power_count)]
        before, now = jnp.ones_like(g), g
        for k in range(2, term_count):
            before, now = now, twice * now - before
            for j in range(power_count):
                for c in range(2):
                    sums[j][c] = sums[j][c] + coef_ref[c, k, j] * now
        for j in range(power_count):
            for c in range(2):
                out_ref[j, c, rows, :] = sums[j][c]
        return carry

    lax.fori_loop(0, left_ref.shape[0] // block, rows_step, 0)


def spectral_factors(poly_coef, nx, ny):
    return pl.pallas_call(
        factors_kernel,
        out_shape=pltpu.HBM((poly_coef.shape[2], 2, nx, ny), jnp.float32),
        in_specs=[SMEM, VMEM, VMEM],
        out_specs=VMEM,
        compiler_params=pltpu.CompilerParams(vmem_limit_bytes=6 * 1024 * 1024),
        cost_estimate=pl.CostEstimate(
            flops=poly_coef.size * 2 * nx * ny, bytes_accessed=32 * nx * ny, transcendentals=0
        ),
        name="spectral_factors",
    )(
        poly_coef,
        jnp.asarray(eigenvalues(nx)[:, None], jnp.float32),
        jnp.asarray(eigenvalues(ny)[None, :], jnp.float32),
    )


def first_kernel(
    left_ref, right_ref, order_x_ref, order_y_ref, factor_hbm, start_ref, part_ref, spectrum, columns, factor_ref, sem
):
    fetch = pltpu.make_async_copy(factor_hbm, factor_ref, sem)
    fetch.start()
    for c in range(2):
        spectrum[c] = forward(reorder(start_ref[c], order_x_ref[...], order_y_ref[...]), left_ref, right_ref)
    fetch.wait()
    half_parts(left_ref, factor_ref, spectrum, columns, range(2))
    for j in range(part_ref.shape[0]):
        for c in range(2):
            part_ref[j, c] = inverse_y(columns[j, c], right_ref)


def first_parts(left, right, order_x, order_y, factors, start):
    power_count, _, nx, ny = factors.shape
    return pl.pallas_call(
        first_kernel,
        out_shape=pltpu.VMEM((power_count, 2, nx, ny), jnp.float32),
        in_specs=[VMEM, VMEM, VMEM, VMEM, HBM, VMEM],
        out_specs=VMEM,
        scratch_shapes=[
            pltpu.VMEM((2, nx, ny), jnp.float32),
            pltpu.VMEM(factors.shape, jnp.float32),
            pltpu.VMEM(factors.shape, jnp.float32),
            pltpu.SemaphoreType.DMA,
        ],
        compiler_params=pltpu.CompilerParams(vmem_limit_bytes=10 * 1024 * 1024),
        cost_estimate=pl.CostEstimate(
            flops=80 * nx * ny * (nx + ny) // 2, bytes_accessed=64 * nx * ny, transcendentals=0
        ),
        name="first_parts",
    )(left, right, order_x, order_y, in_hbm(factors), start)


def depth_kernel(
    slot_ref, place_ref, left_hbm, right_hbm, factor_hbm, part_ref, speed_ref,
    keep_ref, send_ref, spectrum, real_ref, slow, state, columns, left_ref, right_ref, factor_ref, sems,
    *, total_freq,
):
    _, chips, depth_count, local_x, _ = speed_ref.shape
    power_count = factor_ref.shape[0]
    nx, ny = slow.shape
    image_scale = 1.0 / math.sqrt(total_freq)
    scale = (slot_ref[place_ref[0]] + 1).astype(jnp.float32) / total_freq
    core = lax.rem(place_ref[0], 2)

    def rows_of(chip, number):
        block = 2 * chip + number
        if block >= chips:
            block = 3 * chips - 1 - block
        return slice(block * local_x, (block + 1) * local_x)

    def load_slow(z):
        for number in range(2):
            @pl.when(core == number)
            def _():
                for chip in range(chips):
                    slow[rows_of(chip, number), :] = scale / speed_ref[0, chip, z].astype(jnp.float32)
                    slow[rows_of(chip, 1 - number), :] = scale / speed_ref[1, chip, z].astype(jnp.float32)

    def store_image(z):
        half = ny // 2
        for number in range(2):
            @pl.when(core == number)
            def _():
                for chip in range(chips):
                    for side in range(2):
                        lanes = slice(side * half, (side + 1) * half)
                        keep_ref[chip, 2 * z + side] = state[0, rows_of(chip, number), lanes] * image_scale
                        send_ref[chip, 2 * z + side] = state[0, rows_of(chip, 1 - number), lanes] * image_scale

    sides = [
        pltpu.make_async_copy(right_hbm, right_ref, sems.at[0]),
        pltpu.make_async_copy(left_hbm, left_ref, sems.at[1]),
    ]
    fetch = pltpu.make_async_copy(factor_hbm, factor_ref, sems.at[2])
    for copy in sides:
        copy.start()
    fetch.start()
    load_slow(0)
    for c in range(2):
        total = part_ref[power_count - 1, c]
        for j in range(power_count - 2, -1, -1):
            total = total * slow[...] + part_ref[j, c]
        state[c] = total
    store_image(0)

    for copy in sides:
        copy.wait()

    def to_spectrum(z):
        load_slow(z)
        for c in range(2):
            spectrum[c] = forward(state[c], left_ref, right_ref)

        @pl.when(z == 1)
        def _():
            fetch.wait()

    def depth_step(z, carry):
        to_spectrum(z)
        half_parts(left_ref, factor_ref, spectrum, columns, range(2))
        sum_powers(right_ref, columns, slow, state, range(2))
        store_image(z)
        return carry

    lax.fori_loop(1, depth_count - 1, depth_step, 0)
    to_spectrum(depth_count - 1)
    half_parts(left_ref, factor_ref, spectrum, columns, range(1))
    sum_powers(right_ref, columns, slow, state, range(1))
    store_image(depth_count - 1)
    real_ref[...] = state[0]
    shares = 2 * depth_count
    peak = jnp.max(jnp.abs(keep_ref[:, :shares]), axis=(0, 1))
    peak = jnp.maximum(peak, jnp.max(jnp.abs(send_ref[:, :shares]), axis=(0, 1)))
    peak = jnp.max(jnp.max(peak, axis=0, keepdims=True), axis=1, keepdims=True)
    for chip in range(chips):
        keep_ref[chip, shares] = jnp.broadcast_to(peak, keep_ref.shape[2:])
        send_ref[chip, shares] = jnp.broadcast_to(peak, keep_ref.shape[2:])


def depth_steps(freq_slot, place, left, right, factors, parts, speed):
    _, chips, depth_count, local_x, ny = speed.shape
    nx = factors.shape[2]

    def kernel(*refs):
        depth_kernel(*refs, total_freq=freq_slot.shape[0])

    share = jax.ShapeDtypeStruct((chips, 2 * depth_count + 1, local_x, ny // 2), jnp.float32)
    field = jax.ShapeDtypeStruct((nx, ny), jnp.float32)
    return pl.pallas_call(
        kernel,
        out_shape=(share, share, jax.ShapeDtypeStruct((2, nx, ny), jnp.float32), field, field),
        in_specs=[SMEM, SMEM, HBM, HBM, HBM, VMEM, VMEM],
        out_specs=(VMEM,) * 5,
        scratch_shapes=[
            pltpu.VMEM((2, nx, ny), jnp.float32),
            pltpu.VMEM(factors.shape, jnp.float32),
            pltpu.VMEM(left.shape, jnp.bfloat16),
            pltpu.VMEM(right.shape, jnp.bfloat16),
            pltpu.VMEM(factors.shape, jnp.float32),
            pltpu.SemaphoreType.DMA((3,)),
        ],
        compiler_params=pltpu.CompilerParams(vmem_limit_bytes=12 * 1024 * 1024),
        cost_estimate=pl.CostEstimate(
            flops=depth_count * 80 * nx * ny * (nx + ny) // 2, bytes_accessed=64 * nx * ny, transcendentals=0
        ),
        name="depth_steps",
    )(freq_slot, place, in_hbm(left), in_hbm(right), in_hbm(factors), in_vmem(parts), speed)


def last_kernel(
    left_hbm, right_hbm, order_x_hbm, order_y_hbm, factor_hbm, spectrum, real_ref, slow,
    field_ref, state, columns, left_ref, right_ref, order_x_ref, order_y_ref, factor_ref, sems,
):
    pairs = [
        (order_y_hbm, order_y_ref), (order_x_hbm, order_x_ref), (left_hbm, left_ref), (right_hbm, right_ref),
        (factor_hbm, factor_ref),
    ]
    copies = [pltpu.make_async_copy(source, target, sems.at[i]) for i, (source, target) in enumerate(pairs)]
    for copy in copies:
        copy.start()
    for copy in copies[:2]:
        copy.wait()
    field_ref[0] = reorder(real_ref[...], order_x_ref[...], order_y_ref[...])
    for copy in copies[2:]:
        copy.wait()
    half_parts(left_ref, factor_ref, spectrum, columns, range(1, 2))
    sum_powers(right_ref, columns, slow, state, range(1, 2))
    field_ref[1] = reorder(state[1], order_x_ref[...], order_y_ref[...])


def last_field(left, right, order_x, order_y, factors, spectrum, real, slow):
    _, nx, ny = spectrum.shape
    tables = [left, right, order_x, order_y, factors]
    return pl.pallas_call(
        last_kernel,
        out_shape=jax.ShapeDtypeStruct((2, nx, ny), jnp.float32),
        in_specs=[HBM] * 5 + [VMEM] * 3,
        out_specs=VMEM,
        scratch_shapes=[
            pltpu.VMEM((2, nx, ny), jnp.float32),
            pltpu.VMEM(factors.shape, jnp.float32),
            *(pltpu.VMEM(table.shape, table.dtype) for table in tables),
            pltpu.SemaphoreType.DMA((5,)),
        ],
        compiler_params=pltpu.CompilerParams(vmem_limit_bytes=14 * 1024 * 1024),
        cost_estimate=pl.CostEstimate(
            flops=40 * nx * ny * (nx + ny) // 2, bytes_accessed=64 * nx * ny, transcendentals=0
        ),
        name="last_field",
    )(*(in_hbm(table) for table in tables), spectrum, real, slow)


def spectra_kernel(
    slot_hbm, table_hbm, traces_hbm, speed_hbm, rows_hbm, lanes_hbm,
    out_ref, slot_ref, table_ref, traces_ref, speed_ref, rows_ref, lanes_ref, bins, sems,
):
    slots, _, local_x, ny = out_ref.shape
    chunk = max(local_x // 4, 1)
    pairs = [
        (table_hbm, table_ref), (slot_hbm, slot_ref), (speed_hbm, speed_ref), (lanes_hbm, lanes_ref),
        (rows_hbm, rows_ref),
    ]
    copies = [pltpu.make_async_copy(source, target, sems.at[i]) for i, (source, target) in enumerate(pairs)]
    small = len(copies)
    for i, x in enumerate(range(0, local_x, chunk)):
        part = pl.ds(x, chunk)
        copies.append(pltpu.make_async_copy(traces_hbm.at[part], traces_ref.at[part], sems.at[small + i]))
    for copy in copies:
        copy.start()
    for copy in copies[:small]:
        copy.wait()
    speed = dot(rows_ref[...], dot(speed_ref[...], lanes_ref[...]).astype(jnp.bfloat16))
    for f in range(slots):
        out_ref[f, 2] = speed[f * local_x : (f + 1) * local_x]
    for i, x in enumerate(range(0, local_x, chunk)):
        copies[small + i].wait()
        rows = traces_ref[x : x + chunk].reshape(chunk * ny, traces_ref.shape[2])
        result = lax.dot_general(
            table_ref[...], rows, (((1,), (1,)), ((), ())), preferred_element_type=jnp.float32
        )
        for k in range(chunk):
            bins[:, x + k, :] = result[:, k * ny : (k + 1) * ny]
    for f in range(slots):
        for c in range(2):
            out_ref[f, c] = bins[2 * slot_ref[f] + c] * SPECTRA_SCALE


def position_spectra(freq_slot, traces, speed):
    local_x, ny, sample_count = traces.shape
    slots = freq_slot.shape[0]
    nx = speed.shape[0]
    index = np.arange(1, slots + 1)[:, None] * np.arange(sample_count)[None, :] % sample_count
    phases = index.astype(np.float32) * np.float32(2.0 * math.pi / sample_count)
    table = np.stack([np.cos(phases), -np.sin(phases)], axis=1) / np.float32(math.sqrt(sample_count))
    table = jnp.asarray(table.reshape(2 * slots, sample_count).astype(jnp.bfloat16))
    order = np.arange(nx).reshape(-1, local_x)
    order[order.shape[0] // 2 :] = order[order.shape[0] // 2 :, ::-1]
    rows = jnp.asarray(np.eye(nx)[order.reshape(-1)].astype(jnp.bfloat16))
    lanes = jnp.asarray(fold_matrix(ny))
    chunk = max(local_x // 4, 1)
    return pl.pallas_call(
        spectra_kernel,
        out_shape=jax.ShapeDtypeStruct((slots, 3, local_x, ny), jnp.float32),
        in_specs=[HBM] * 6,
        out_specs=VMEM,
        scratch_shapes=[
            pltpu.SMEM((slots,), jnp.int32),
            pltpu.VMEM((2 * slots, sample_count), jnp.bfloat16),
            pltpu.VMEM(traces.shape, jnp.bfloat16),
            pltpu.VMEM(speed.shape, jnp.bfloat16),
            pltpu.VMEM((nx, nx), jnp.bfloat16),
            pltpu.VMEM((ny, ny), jnp.bfloat16),
            pltpu.VMEM((2 * slots, local_x, ny), jnp.float32),
            pltpu.SemaphoreType.DMA((5 + local_x // chunk,)),
        ],
        compiler_params=pltpu.CompilerParams(vmem_limit_bytes=8 * 1024 * 1024),
        cost_estimate=pl.CostEstimate(
            flops=4 * slots * traces.size, bytes_accessed=2 * traces.size, transcendentals=0
        ),
        name="position_spectra",
    )(in_hbm(freq_slot), in_hbm(table), in_hbm(traces), in_hbm(speed), in_hbm(rows), in_hbm(lanes))


def exact_dot(a, b):
    return jnp.dot(a, b, preferred_element_type=jnp.float32, precision=lax.Precision.HIGHEST)


def image_kernel(place_ref, lanes_ref, rows_ref, share_ref, image_ref):
    depth_count, local_x, ny = image_ref.shape
    half = ny // 2
    total = jnp.sum(share_ref[:, : 2 * depth_count] * jnp.exp2(share_ref[:, 2 * depth_count :]), axis=0)
    turned = exact_dot(
        jnp.concatenate([total[2 * z + 1] for z in range(depth_count)], axis=0), lanes_ref[...]
    )
    image = jnp.concatenate(
        [jnp.concatenate([total[2 * z] for z in range(depth_count)], axis=0), turned], axis=1
    )
    upper = place_ref[0] >= share_ref.shape[0]

    @pl.when(upper)
    def _():
        image_ref[...] = exact_dot(rows_ref[...], image).reshape(image_ref.shape)

    @pl.when(jnp.logical_not(upper))
    def _():
        image_ref[...] = image.reshape(image_ref.shape)


def image_rows(place, shares):
    _, parts, local_x, half = shares.shape
    depth_count = parts // 2
    lanes = jnp.asarray(np.eye(half)[::-1], jnp.float32)
    rows = jnp.asarray(np.kron(np.eye(depth_count), np.eye(local_x)[::-1]), jnp.float32)
    return pl.pallas_call(
        image_kernel,
        out_shape=jax.ShapeDtypeStruct((depth_count, local_x, 2 * half), jnp.float32),
        in_specs=[SMEM, VMEM, VMEM, VMEM],
        out_specs=VMEM,
        compiler_params=pltpu.CompilerParams(vmem_limit_bytes=4 * 1024 * 1024),
        name="image_rows",
    )(place, lanes, rows, shares)


def swap_cores(array, count):
    return lax.ppermute(array, "freq", [(i, i ^ 1) for i in range(count)])


def on_device(traces, velocity, poly_coef, freq_slot, depth_owner):
    devices = lax.axis_size("freq")
    local_x, ny, _ = traces.shape
    nx = devices * local_x
    chips = devices // 2
    depth_count = depth_owner.shape[0]
    place = lax.axis_index("freq").astype(jnp.int32).reshape(1)
    same_core = [[i for i in range(devices) if i % 2 == c] for c in range(2)]

    spectra = position_spectra(freq_slot, traces, velocity.reshape(nx, ny))
    received = lax.all_to_all(
        spectra.astype(jnp.float16), "freq", split_axis=0, concat_axis=0, tiled=True
    )
    received, factors = lax.optimization_barrier((received, spectral_factors(poly_coef, nx, ny)))
    start = received[:, :2].transpose(1, 0, 2, 3).reshape(2, nx, ny).astype(jnp.float32) / SPECTRA_SCALE

    owned = (depth_owner[:, None] == jnp.arange(devices, dtype=jnp.int32)[None, :]).astype(jnp.bfloat16)
    by_rows = received[:, 2].astype(jnp.bfloat16).reshape(devices, local_x * ny)
    chosen = jnp.dot(owned, by_rows, preferred_element_type=jnp.float32).astype(jnp.bfloat16)
    chosen = jnp.broadcast_to(
        chosen.reshape(1, depth_count, local_x, ny), (chips, depth_count, local_x, ny)
    )
    mine = lax.all_to_all(
        chosen, "freq", split_axis=0, concat_axis=0, tiled=True, axis_index_groups=same_core
    )
    left = jnp.asarray(np.swapaxes(right_matrices(nx), 1, 2))
    right = jnp.asarray(right_matrices(ny))
    order_x, order_y = jnp.asarray(fold_matrix(nx)), jnp.asarray(fold_matrix(ny))
    parts = first_parts(left, right, order_x, order_y, factors, start)
    parts, mine = lax.optimization_barrier((parts, mine))
    speed = jnp.stack([mine, swap_cores(mine, devices)])
    keep, send, spectrum, real, slow = depth_steps(
        freq_slot, place, left, right, factors, parts, speed
    )

    total = keep + swap_cores(send, devices)
    power = jnp.ceil(jnp.log2(jnp.maximum(total[:, 2 * depth_count :], 1e-30)))
    packed = jnp.concatenate([total[:, : 2 * depth_count] * jnp.exp2(-power), power], axis=1)
    shares = lax.all_to_all(
        packed.astype(jnp.float16),
        "freq",
        split_axis=0,
        concat_axis=0,
        tiled=True,
        axis_index_groups=same_core,
    )
    wavefield = last_field(left, right, order_x, order_y, factors, spectrum, real, slow)
    shares, wavefield = lax.optimization_barrier((shares, wavefield))
    return (image_rows(place, shares.astype(jnp.float32)), wavefield[:, None])


def solution(mesh):
    return jax.shard_map(
        on_device,
        mesh=mesh,
        in_specs=(
            P(("group", "freq"), None, None),
            P(("group", "freq"), None, None),
            P(),
            P(),
            P("group"),
        ),
        out_specs=(P(None, ("group", "freq"), None), P(None, ("group", "freq"), None, None)),
        check_vma=False,
    )
```

time: 69 us -> 65.3 us (0.946)
  blocking collectives: 14.6 us -> 0 us
  waiting for transfers between devices: 16.6 us -> 22.8 us
  starting transfers between devices: 11 us -> 14.6 us
  Pallas kernels: 22.3 us -> 23.5 us
    all_to_all x1 -> x0, blocking collectives: 14.6 us -> none  [on_device(): lax.all_to_all(packed.astype(jnp.float16), 'freq', split_axis=0, concat_a...]
    all_to_all x0 -> x1, waiting for transfers between devices: none -> 5.65 us  [on_device(): lax.all_to_all(packed.astype(jnp.float16), 'freq', split_axis=0, concat_a...]
    pallas_call x0 -> x2, Pallas kernels: none -> 5.14 us  [the longest x1 4.29 us: last_field(): pl.pallas_call(last_kernel, out_shape=jax.ShapeDtypeStruct((2, nx, ny), j...]
    pallas_call x1, Pallas kernels: 11.7 us -> 8.07 us  [depth_steps(): pl.pallas_call(kernel, out_shape=(share, share, jax.ShapeDtypeStruct((2,...]
    all_to_all x0 -> x1, starting transfers between devices: none -> 3.56 us  [on_device(): lax.all_to_all(packed.astype(jnp.float16), 'freq', split_axis=0, concat_a...]
    concatenate x1, other arithmetic: 0.08 us -> 0.8 us  [on_device(): jnp.concatenate([total[:, :2 * depth_count] * jnp.exp2(-power), power], a...]
  transfers between devices with their start and end apart: 4 -> 5, of which waited for: 4 -> 5; matrix products, arithmetic and copies ran while one was open for 0% -> 0% of each run, Pallas kernels for 12% -> 18%
where the time goes in v2:
time: 65.3 us; the launch traced here: 64.9 us
  Pallas kernels  23.5 us (36%)
  waiting for transfers between devices  22.8 us (35%)
  starting transfers between devices  14.6 us (22%)
  other arithmetic  1.95 us (3%)
  local copies, waits for them, and re-layouts  0.97 us (1%)
  between operations  0.85 us (1%)
    pallas_call x1, Pallas kernels, depth_steps(): pl.pallas_call(kernel, out_shape=(share, share, jax.ShapeDtypeStruct((2,...  8.07 us
    all_to_all x1, waiting for transfers between devices, on_device(): lax.all_to_all(spectra.astype(jnp.float16), 'freq', split_axis=0, concat_...  7.66 us
    all_to_all x1, starting transfers between devices, on_device(): lax.all_to_all(spectra.astype(jnp.float16), 'freq', split_axis=0, concat_...  7.39 us
    all_to_all x1, waiting for transfers between devices, on_device(): lax.all_to_all(chosen, 'freq', split_axis=0, concat_axis=0, tiled=True, a...  6.11 us
    all_to_all x1, waiting for transfers between devices, on_device(): lax.all_to_all(packed.astype(jnp.float16), 'freq', split_axis=0, concat_a...  5.65 us
    pallas_call x1, Pallas kernels, spectral_factors(): pl.pallas_call(factors_kernel, out_shape=pltpu.HBM((poly_coef.shape[2], 2...  4.41 us
    pallas_call x1, Pallas kernels, last_field(): pl.pallas_call(last_kernel, out_shape=jax.ShapeDtypeStruct((2, nx, ny), j...  4.29 us
    all_to_all x1, starting transfers between devices, on_device(): lax.all_to_all(packed.astype(jnp.float16), 'freq', split_axis=0, concat_a...  3.56 us
  transfers between devices with their start and end apart: 5, of which 5 were waited for; matrix products, arithmetic and copies ran while one was open for 0% of the time, Pallas kernels for 18%

profile of v2, /device:TPU:0, one launch (start us, length us, event | category | flops | bytes accessed | tf_op | source)
XLA Modules:
  0.0 64.9 jit_solution(11942168496916858267)
XLA Ops:
  0.6 0.0 copy-start.8
  0.6 0.0 copy-start.3
  0.7 0.0 copy-start.6
  0.7 2.8 %position_spectra.1 = f32[16,3,16,256]{3,2,1,0:T(8,128)S(1)} custom-call(s32[16]{0:T(128)} %refs_0_.1, bf16[32,256]{1,0:T(8,128)(2,1)} %constant.31.clone.table_hbm, bf16[16,256,256]{2,1,0:T(8,128)(2,1)} %traces_hbm.1, bf16[256,256]{1,0:T(8,128)(2,1)} %bitcast.26, bf16[256,256]{1,0:T(8,128)(2,1)} %constant.32.clone.rows_hbm, ...), custom_call_target="tpu_custom_call" | custom-call | flops 67108864 | bytes 2097152 | tf_op jit(solution)/shard_map/position_spectra/pallas_call | solution.py:406
  3.4 0.0 copy-start.9
  3.4 0.8 %convert_element_type.23 = f16[16,3,16,256]{3,2,1,0:T(8,128)(2,1)} convert(f32[16,3,16,256]{3,2,1,0:T(8,128)S(1)} %position_spectra.1) | non-fusion elementwise | flops 196608 | bytes 1179648 | tf_op jit(solution)/shard_map/convert_element_type | solution.py:484
  4.3 7.4 %all-to-all-start = ((f16[16,3,16,256]{3,2,1,0:T(8,128)(2,1)}), f16[16,3,16,256]{3,2,1,0:T(8,128)(2,1)S(1)}, u32[]{:S(2)}, u32[]{:S(2)}) async-start(f16[16,3,16,256]{3,2,1,0:T(8,128)(2,1)} %convert_element_type.23), calls=%async_computation | async-start | bytes 786432 | tf_op jit(solution)/shard_map/all_to_all | solution.py:483
  11.7 0.0 copy-done.8
  11.7 0.1 copy.18.coef_ref
  11.8 4.4 %spectral_factors.1.factor_hbm.refs_4_ = f32[4,2,256,256]{3,2,1,0:T(8,128)} custom-call(f32[2,10,4]{2,1,0:T(8,128)S(1)} %copy.18.coef_ref, f32[256,1]{1,0:T(8,128)S(1)} %copy-done.3, f32[1,256]{1,0:T(1,128)S(1)} %copy-done.6), custom_call_target="tpu_custom_call" | custom-call | flops 10485760 | bytes 2097152 | tf_op jit(solution)/shard_map/spectral_factors/pallas_call | solution.py:146
  16.2 7.7 %all-to-all-done = f16[16,3,16,256]{3,2,1,0:T(8,128)(2,1)S(1)} async-done(((f16[16,3,16,256]{3,2,1,0:T(8,128)(2,1)}), f16[16,3,16,256]{3,2,1,0:T(8,128)(2,1)S(1)}, u32[]{:S(2)}, u32[]{:S(2)}) %all-to-all-start) | async-done | bytes 393248 | tf_op jit(solution)/shard_map/all_to_all | solution.py:483
  23.9 0.2 convolution_convert_fusion
  24.2 0.7 %broadcast_in_dim.13 = bf16[8,4,16,256]{3,2,1,0:T(8,128)(2,1)} broadcast(bf16[4,16,256]{2,1,0:T(8,128)(2,1)S(1)} %bitcast.28), dimensions={1,2,3} | broadcast | bytes 294912 | tf_op jit(solution)/shard_map/broadcast_in_dim | solution.py:492
  24.9 3.4 %all-to-all-start.1 = ((bf16[8,4,16,256]{3,2,1,0:T(8,128)(2,1)}), bf16[8,4,16,256]{3,2,1,0:T(8,128)(2,1)S(1)}, u32[]{:S(2)}, u32[]{:S(2)}) async-start(bf16[8,4,16,256]{3,2,1,0:T(8,128)(2,1)} %broadcast_in_dim.13), calls=%async_computation.1 | async-start | bytes 524288 | tf_op jit(solution)/shard_map/all_to_all | solution.py:495
  28.3 0.1 multiply_bitcast_fusion
  28.4 0.0 copy-start.7
  28.5 3.1 %first_parts.1.refs_5_ = f32[4,2,256,256]{3,2,1,0:T(8,128)S(1)} custom-call(bf16[4,256,256]{2,1,0:T(8,128)(2,1)S(1)} %copy-done.2, bf16[4,256,256]{2,1,0:T(8,128)(2,1)S(1)} %copy-done.1, bf16[256,256]{1,0:T(8,128)(2,1)S(1)} %copy-done, bf16[256,256]{1,0:T(8,128)(2,1)S(1)} %copy-done, f32[4,2,256,256]{3,2,1,0:T(8,128)} %spectral_factors.1.factor_hbm.refs_4_, ...), custom_call_target="tpu_custom_call" | custom-call | flops 1342177280 | bytes 4194304 | tf_op jit(solution)/shard_map/first_parts/pallas_call | solution.py:179
  31.6 6.1 %all-to-all-done.1 = bf16[8,4,16,256]{3,2,1,0:T(8,128)(2,1)S(1)} async-done(((bf16[8,4,16,256]{3,2,1,0:T(8,128)(2,1)}), bf16[8,4,16,256]{3,2,1,0:T(8,128)(2,1)S(1)}, u32[]{:S(2)}, u32[]{:S(2)}) %all-to-all-start.1) | async-done | bytes 262176 | tf_op jit(solution)/shard_map/all_to_all | solution.py:495
  37.7 0.0 collective-permute-start
  37.7 1.5 %collective-permute-done = bf16[8,4,16,256]{3,2,1,0:T(8,128)(2,1)S(1)} collective-permute-done((bf16[8,4,16,256]{3,2,1,0:T(8,128)(2,1)S(1)}, bf16[8,4,16,256]{3,2,1,0:T(8,128)(2,1)S(1)}, u32[]{:S(2)}, u32[]{:S(2)}) %collective-permute-start) | collective-permute-done | bytes 262176 | tf_op jit(solution)/shard_map/ppermute | solution.py:470
  39.3 0.1 pad_maximum_fusion.refs_6_
  39.3 8.1 %depth_steps.1 = (f32[8,9,16,128]{3,2,1,0:T(8,128)S(1)}, f32[8,9,16,128]{3,2,1,0:T(8,128)S(1)}, f32[2,256,256]{2,1,0:T(8,128)S(1)}, f32[256,256]{1,0:T(8,128)S(1)}, f32[256,256]{1,0:T(8,128)S(1)}) custom-call(s32[16]{0:T(128)S(1)} %copy-done.7, s32[1]{0:T(128)} %bitcast.refs_1_.place_ref, bf16[4,256,256]{2,1,0:T(8,128)(2,1)} %constant.36.clone.left_ref.refs_2_.left_hbm, ...), custom_call_target="tpu_custom_call" | custom-call | flops 5368709120 | bytes 4194304 | tf_op jit(solution)/shard_map/depth_steps/pallas_call | solution.py:294
  47.4 0.2 collective-permute-start.1
  47.6 1.8 %collective-permute-done.1 = f32[8,9,16,128]{3,2,1,0:T(8,128)S(1)} collective-permute-done((f32[8,9,16,128]{3,2,1,0:T(8,128)S(1)}, f32[8,9,16,128]{3,2,1,0:T(8,128)S(1)}, u32[]{:S(2)}, u32[]{:S(2)}) %collective-permute-start.1) | collective-permute-done | bytes 589856 | tf_op jit(solution)/shard_map/ppermute | solution.py:470
  49.5 0.1 add.3
  49.6 0.1 fusion
  49.7 0.8 %pad_maximum_fusion.1 = f16[8,9,16,128]{3,2,1,0:T(8,128)(2,1)} fusion(f16[8,1,16,128]{3,2,1,0:T(8,128)(2,1)S(1)} %get-tuple-element.27, f16[8,8,16,128]{3,2,1,0:T(8,128)(2,1)S(1)} %fusion), kind=kLoop, calls=%fused_computation.5 | loop fusion | flops 147456 | bytes 589824 | tf_op jit(solution)/shard_map/concatenate | solution.py:510
  50.5 3.6 %all-to-all-start.2 = ((f16[8,9,16,128]{3,2,1,0:T(8,128)(2,1)}), f16[8,9,16,128]{3,2,1,0:T(8,128)(2,1)S(1)}, u32[]{:S(2)}, u32[]{:S(2)}) async-start(f16[8,9,16,128]{3,2,1,0:T(8,128)(2,1)} %pad_maximum_fusion.1), calls=%async_computation.2 | async-start | bytes 589824 | tf_op jit(solution)/shard_map/all_to_all | solution.py:511
  54.0 0.0 copy-start.5
  54.0 4.3 %last_field.1 = f32[2,256,256]{2,1,0:T(8,128)} custom-call(bf16[4,256,256]{2,1,0:T(8,128)(2,1)} %constant.36.clone.left_ref.refs_2_.left_hbm, bf16[4,256,256]{2,1,0:T(8,128)(2,1)} %constant.37.clone.right_ref.refs_3_.right_hbm, bf16[256,256]{1,0:T(8,128)(2,1)} %constant.33.clone.lanes_hbm.order_x_ref.order_y_ref.order_x_hbm.order_y_hbm, ...), custom_call_target="tpu_custom_call" | custom-call | flops 671088640 | bytes 4194304 | tf_op jit(solution)/shard_map/last_field/pallas_call | solution.py:339
  58.3 5.6 %all-to-all-done.2 = f16[8,9,16,128]{3,2,1,0:T(8,128)(2,1)S(1)} async-done(((f16[8,9,16,128]{3,2,1,0:T(8,128)(2,1)}), f16[8,9,16,128]{3,2,1,0:T(8,128)(2,1)S(1)}, u32[]{:S(2)}, u32[]{:S(2)}) %all-to-all-start.2) | async-done | bytes 294944 | tf_op jit(solution)/shard_map/all_to_all | solution.py:511
  64.0 0.8 %image_rows.1 = f32[4,16,256]{2,1,0:T(8,128)} custom-call(s32[1]{0:T(128)} %bitcast.refs_1_.place_ref, f32[128,128]{1,0:T(8,128)S(1)} %copy-done.4, f32[64,64]{1,0:T(8,128)S(1)} %copy-done.5, f32[8,9,16,128]{3,2,1,0:T(8,128)S(1)} %convert_element_type.28.share_ref), custom_call_target="tpu_custom_call" | custom-call | tf_op jit(solution)/shard_map/image_rows/pallas_call | solution.py:459
  (19 shorter events, 0.2 us)
Async XLA Ops:
  0.6 11.0 %copy-start.8 = (f32[2,10,4]{1,2,0:T(4,128)S(1)}, f32[2,10,4]{1,2,0:T(4,128)}, u32[]{:S(2)}) copy-start(f32[2,10,4]{1,2,0:T(4,128)} %param.18) | copy-start | bytes 964
  0.6 11.1 %copy-start.3 = (f32[256,1]{1,0:T(8,128)S(1)}, f32[256,1]{1,0:T(8,128)}, u32[]{:S(2)}) copy-start(f32[256,1]{1,0:T(8,128)} %constant.34.clone.left_ref) | copy-start | bytes 3076
  0.7 11.1 %copy-start.6 = (f32[1,256]{1,0:T(1,128)S(1)}, f32[1,256]{1,0:T(1,128)}, u32[]{:S(2)}) copy-start(f32[1,256]{1,0:T(1,128)} %constant.35.clone.right_ref) | copy-start | bytes 3076
  3.4 20.5 %copy-start.9 = (s32[4]{0:T(128)S(1)}, s32[4]{0:T(128)}, u32[]{:S(2)}) copy-start(s32[4]{0:T(128)} %param.20) | copy-start | bytes 52
  4.3 19.6 %all-to-all-start = ((f16[16,3,16,256]{3,2,1,0:T(8,128)(2,1)}), f16[16,3,16,256]{3,2,1,0:T(8,128)(2,1)S(1)}, u32[]{:S(2)}, u32[]{:S(2)}) async-start(f16[16,3,16,256]{3,2,1,0:T(8,128)(2,1)} %convert_element_type.23), calls=%async_computation | async-start | bytes 786432 | tf_op jit(solution)/shard_map/all_to_all | solution.py:483
  16.2 12.2 %copy-start = (bf16[256,256]{1,0:T(8,128)(2,1)S(1)}, bf16[256,256]{1,0:T(8,128)(2,1)}, u32[]{:S(2)}) copy-start(bf16[256,256]{1,0:T(8,128)(2,1)} %constant.33.clone.lanes_hbm.order_x_ref.order_y_ref.order_x_hbm.order_y_hbm) | copy-start | bytes 393220
  16.2 12.2 %copy-start.1 = (bf16[4,256,256]{2,1,0:T(8,128)(2,1)S(1)}, bf16[4,256,256]{2,1,0:T(8,128)(2,1)}, u32[]{:S(2)}) copy-start(bf16[4,256,256]{2,1,0:T(8,128)(2,1)} %constant.37.clone.right_ref.refs_3_.right_hbm) | copy-start | bytes 1572868
  16.2 12.3 %copy-start.2 = (bf16[4,256,256]{2,1,0:T(8,128)(2,1)S(1)}, bf16[4,256,256]{2,1,0:T(8,128)(2,1)}, u32[]{:S(2)}) copy-start(bf16[4,256,256]{2,1,0:T(8,128)(2,1)} %constant.36.clone.left_ref.refs_2_.left_hbm) | copy-start | bytes 1572868
  24.9 12.8 %all-to-all-start.1 = ((bf16[8,4,16,256]{3,2,1,0:T(8,128)(2,1)}), bf16[8,4,16,256]{3,2,1,0:T(8,128)(2,1)S(1)}, u32[]{:S(2)}, u32[]{:S(2)}) async-start(bf16[8,4,16,256]{3,2,1,0:T(8,128)(2,1)} %broadcast_in_dim.13), calls=%async_computation.1 | async-start | bytes 524288 | tf_op jit(solution)/shard_map/all_to_all | solution.py:495
  28.4 10.9 %copy-start.7 = (s32[16]{0:T(128)S(1)}, s32[16]{0:T(128)}, u32[]{:S(2)}) copy-start(s32[16]{0:T(128)} %refs_0_.1) | copy-start | bytes 196
  37.7 1.5 %collective-permute-start = (bf16[8,4,16,256]{3,2,1,0:T(8,128)(2,1)S(1)}, bf16[8,4,16,256]{3,2,1,0:T(8,128)(2,1)S(1)}, u32[]{:S(2)}, u32[]{:S(2)}) collective-permute-start(bf16[8,4,16,256]{3,2,1,0:T(8,128)(2,1)S(1)} %all-to-all-done.1), channel_id=1, source_target_pairs={{0,1},{1,0},{2,3},{3,2},{4,5},{5,4},{6,7},{7,6},{8,9},{9,8},{10,11... | collective-permute-start | bytes 786440 | tf_op jit(solution)/shard_map/ppermute | solution.py:470
  47.4 2.1 %collective-permute-start.1 = (f32[8,9,16,128]{3,2,1,0:T(8,128)S(1)}, f32[8,9,16,128]{3,2,1,0:T(8,128)S(1)}, u32[]{:S(2)}, u32[]{:S(2)}) collective-permute-start(f32[8,9,16,128]{3,2,1,0:T(8,128)S(1)} %get-tuple-element.18), channel_id=1, source_target_pairs={{0,1},{1,0},{2,3},{3,2},{4,5},{5,4},{6,7},{7,6},{8,9},{9,8},{10,11... | collective-permute-start | bytes 1769480 | tf_op jit(solution)/shard_map/ppermute | solution.py:470
  50.5 13.5 %all-to-all-start.2 = ((f16[8,9,16,128]{3,2,1,0:T(8,128)(2,1)}), f16[8,9,16,128]{3,2,1,0:T(8,128)(2,1)S(1)}, u32[]{:S(2)}, u32[]{:S(2)}) async-start(f16[8,9,16,128]{3,2,1,0:T(8,128)(2,1)} %pad_maximum_fusion.1), calls=%async_computation.2 | async-start | bytes 589824 | tf_op jit(solution)/shard_map/all_to_all | solution.py:511
  54.0 10.0 %copy-start.4 = (f32[128,128]{1,0:T(8,128)S(1)}, f32[128,128]{1,0:T(8,128)}, u32[]{:S(2)}) copy-start(f32[128,128]{1,0:T(8,128)} %constant.38.clone.lanes_ref) | copy-start | bytes 196612
  54.0 10.0 %copy-start.5 = (f32[64,64]{1,0:T(8,128)S(1)}, f32[64,64]{1,0:T(8,128)}, u32[]{:S(2)}) copy-start(f32[64,64]{1,0:T(8,128)} %constant.39.clone.rows_ref) | copy-start | bytes 49156

commit v3 on v2

--- a/solution.py
+++ b/solution.py
@@ -1,3 +1,4 @@
+import functools
 import math
 
 import jax
@@ -9,9 +10,23 @@
 from jax.sharding import PartitionSpec as P
 
 SPECTRA_SCALE = 512.0
+SUBLANES = 8
+CHUNK = 128
 SMEM = pl.BlockSpec(memory_space=pltpu.SMEM)
 VMEM = pl.BlockSpec(memory_space=pltpu.VMEM)
 HBM = pl.BlockSpec(memory_space=pltpu.HBM)
+
+
+def device_order(devices):
+    length = devices // 4
+    along = list(range(length // 2, -1, -1)) + list(range(length // 2 + 1, length))
+    return [4 * z + 2 * y + core for y in (1, 0) for z in along for core in (1, 0)]
+
+
+def chip_order(chips):
+    length = chips // 2
+    along = list(range(length // 2, length)) + list(range(length // 2 - 1, -1, -1))
+    return [2 * z + y for y in (0, 1) for z in along]
 
 
 def in_vmem(array):
@@ -111,12 +126,20 @@
             columns[j, c] = inverse_x(mixed, left_ref)
 
 
-def sum_powers(right_ref, columns, slow, state, parts):
-    power_count = columns.shape[0]
-    for j in range(power_count - 1, -1, -1):
-        for c in parts:
-            part = inverse_y(columns[j, c], right_ref)
-            state[c] = part if j == power_count - 1 else state[c] * slow[...] + part
+def sum_powers(right_ref, columns, slow, state, parts, chunk):
+    power_count, _, nx, ny = columns.shape
+    half = ny // 2
+    for c in parts:
+        for first in range(0, nx, chunk):
+            rows = slice(first, first + chunk)
+            stacked = jnp.concatenate([columns[j, c, rows, :] for j in range(power_count)], axis=0)
+            even, odd = along_y(stacked[:, :half], right_ref[2]), along_y(stacked[:, half:], right_ref[3])
+            low, high = even + odd, even - odd
+            for values, lanes in ((low, slice(0, half)), (high, slice(half, ny))):
+                total = values[(power_count - 1) * chunk :]
+                for j in range(power_count - 2, -1, -1):
+                    total = total * slow[rows, lanes] + values[j * chunk : (j + 1) * chunk]
+                state[c, rows, lanes] = total
 
 
 def factors_kernel(coef_ref, left_ref, right_ref, out_ref):
@@ -209,28 +232,38 @@
 
     def rows_of(chip, number):
         block = 2 * chip + number
-        if block >= chips:
+        if 2 * chip >= chips:
             block = 3 * chips - 1 - block
-        return slice(block * local_x, (block + 1) * local_x)
+        if isinstance(block, int):
+            return slice(block * local_x, (block + 1) * local_x)
+        return pl.ds(pl.multiple_of(block * local_x, local_x), local_x)
+
+    def on_core(act):
+        if local_x % SUBLANES == 0:
+            act(core, 1 - core)
+        else:
+            for number in range(2):
+                pl.when(core == number)(functools.partial(act, number, 1 - number))
 
     def load_slow(z):
-        for number in range(2):
-            @pl.when(core == number)
-            def _():
-                for chip in range(chips):
-                    slow[rows_of(chip, number), :] = scale / speed_ref[0, chip, z].astype(jnp.float32)
-                    slow[rows_of(chip, 1 - number), :] = scale / speed_ref[1, chip, z].astype(jnp.float32)
+        def act(own, other):
+            for i, chip in enumerate(chip_order(chips)):
+                slow[rows_of(chip, own), :] = scale / speed_ref[0, i, z].astype(jnp.float32)
+                slow[rows_of(chip, other), :] = scale / speed_ref[1, i, z].astype(jnp.float32)
+
+        on_core(act)
 
     def store_image(z):
         half = ny // 2
-        for number in range(2):
-            @pl.when(core == number)
-            def _():
-                for chip in range(chips):
-                    for side in range(2):
-                        lanes = slice(side * half, (side + 1) * half)
-                        keep_ref[chip, 2 * z + side] = state[0, rows_of(chip, number), lanes] * image_scale
-                        send_ref[chip, 2 * z + side] = state[0, rows_of(chip, 1 - number), lanes] * image_scale
+
+        def act(own, other):
+            for i, chip in enumerate(chip_order(chips)):
+                for side in range(2):
+                    lanes = slice(side * half, (side + 1) * half)
+                    keep_ref[i, 2 * z + side] = state[0, rows_of(chip, own), lanes] * image_scale
+                    send_ref[i, 2 * z + side] = state[0, rows_of(chip, other), lanes] * image_scale
+
+        on_core(act)
 
     sides = [
         pltpu.make_async_copy(right_hbm, right_ref, sems.at[0]),
@@ -251,27 +284,17 @@
     for copy in sides:
         copy.wait()
 
-    def to_spectrum(z):
+    for z in range(1, depth_count):
+        last = z == depth_count - 1
         load_slow(z)
         for c in range(2):
             spectrum[c] = forward(state[c], left_ref, right_ref)
-
-        @pl.when(z == 1)
-        def _():
+        if z == 1:
             fetch.wait()
-
-    def depth_step(z, carry):
-        to_spectrum(z)
-        half_parts(left_ref, factor_ref, spectrum, columns, range(2))
-        sum_powers(right_ref, columns, slow, state, range(2))
+        parts = range(1) if last else range(2)
+        half_parts(left_ref, factor_ref, spectrum, columns, parts)
+        sum_powers(right_ref, columns, slow, state, parts, CHUNK)
         store_image(z)
-        return carry
-
-    lax.fori_loop(1, depth_count - 1, depth_step, 0)
-    to_spectrum(depth_count - 1)
-    half_parts(left_ref, factor_ref, spectrum, columns, range(1))
-    sum_powers(right_ref, columns, slow, state, range(1))
-    store_image(depth_count - 1)
     real_ref[...] = state[0]
     shares = 2 * depth_count
     peak = jnp.max(jnp.abs(keep_ref[:, :shares]), axis=(0, 1))
@@ -329,7 +352,7 @@
     for copy in copies[2:]:
         copy.wait()
     half_parts(left_ref, factor_ref, spectrum, columns, range(1, 2))
-    sum_powers(right_ref, columns, slow, state, range(1, 2))
+    sum_powers(right_ref, columns, slow, state, range(1, 2), CHUNK)
     field_ref[1] = reorder(state[1], order_x_ref[...], order_y_ref[...])
 
 
@@ -375,8 +398,9 @@
     for copy in copies[:small]:
         copy.wait()
     speed = dot(rows_ref[...], dot(speed_ref[...], lanes_ref[...]).astype(jnp.bfloat16))
-    for f in range(slots):
-        out_ref[f, 2] = speed[f * local_x : (f + 1) * local_x]
+    order = device_order(slots)
+    for i, f in enumerate(order):
+        out_ref[i, 2] = speed[f * local_x : (f + 1) * local_x]
     for i, x in enumerate(range(0, local_x, chunk)):
         copies[small + i].wait()
         rows = traces_ref[x : x + chunk].reshape(chunk * ny, traces_ref.shape[2])
@@ -385,9 +409,9 @@
         )
         for k in range(chunk):
             bins[:, x + k, :] = result[:, k * ny : (k + 1) * ny]
-    for f in range(slots):
+    for i, f in enumerate(order):
         for c in range(2):
-            out_ref[f, c] = bins[2 * slot_ref[f] + c] * SPECTRA_SCALE
+            out_ref[i, c] = bins[2 * slot_ref[f] + c] * SPECTRA_SCALE
 
 
 def position_spectra(freq_slot, traces, speed):
@@ -477,16 +501,23 @@
     chips = devices // 2
     depth_count = depth_owner.shape[0]
     place = lax.axis_index("freq").astype(jnp.int32).reshape(1)
-    same_core = [[i for i in range(devices) if i % 2 == c] for c in range(2)]
+    order = device_order(devices)
+    same_core = [[2 * chip + core for chip in chip_order(chips)] for core in range(2)]
 
     spectra = position_spectra(freq_slot, traces, velocity.reshape(nx, ny))
     received = lax.all_to_all(
-        spectra.astype(jnp.float16), "freq", split_axis=0, concat_axis=0, tiled=True
-    )
-    received, factors = lax.optimization_barrier((received, spectral_factors(poly_coef, nx, ny)))
+        spectra.astype(jnp.float16),
+        "freq",
+        split_axis=0,
+        concat_axis=0,
+        tiled=True,
+        axis_index_groups=[order],
+    )
+    received, poly_coef = lax.optimization_barrier((received, poly_coef))
+    factors = spectral_factors(poly_coef, nx, ny)
     start = received[:, :2].transpose(1, 0, 2, 3).reshape(2, nx, ny).astype(jnp.float32) / SPECTRA_SCALE
 
-    owned = (depth_owner[:, None] == jnp.arange(devices, dtype=jnp.int32)[None, :]).astype(jnp.bfloat16)
+    owned = (depth_owner[:, None] == jnp.asarray(order, jnp.int32)[None, :]).astype(jnp.bfloat16)
     by_rows = received[:, 2].astype(jnp.bfloat16).reshape(devices, local_x * ny)
     chosen = jnp.dot(owned, by_rows, preferred_element_type=jnp.float32).astype(jnp.bfloat16)
     chosen = jnp.broadcast_to(
@@ -498,7 +529,8 @@
     left = jnp.asarray(np.swapaxes(right_matrices(nx), 1, 2))
     right = jnp.asarray(right_matrices(ny))
     order_x, order_y = jnp.asarray(fold_matrix(nx)), jnp.asarray(fold_matrix(ny))
-    parts = first_parts(left, right, order_x, order_y, factors, start)
+    arrived = (np.array(order)[:, None] * local_x + np.arange(local_x)).reshape(-1)
+    parts = first_parts(left, right, jnp.asarray(fold_matrix(nx)[:, arrived]), order_y, factors, start)
     parts, mine = lax.optimization_barrier((parts, mine))
     speed = jnp.stack([mine, swap_cores(mine, devices)])
     keep, send, spectrum, real, slow = depth_steps(

time: 65.3 us -> 61.4 us (0.940)
  waiting for transfers between devices: 22.8 us -> 5.81 us
  blocking collectives: 0 us -> 16.2 us
  starting transfers between devices: 14.6 us -> 11.9 us
  Pallas kernels: 23.5 us -> 22.8 us
    all_to_all x0 -> x1, blocking collectives: none -> 16.2 us  [on_device(): lax.all_to_all(spectra.astype(jnp.float16), 'freq', split_axis=0, concat_...]
    all_to_all x1 -> x0, waiting for transfers between devices: 7.66 us -> none  [on_device(): lax.all_to_all(spectra.astype(jnp.float16), 'freq', split_axis=0, concat_...]
    all_to_all x1 -> x0, starting transfers between devices: 7.39 us -> none  [on_device(): lax.all_to_all(spectra.astype(jnp.float16), 'freq', split_axis=0, concat_...]
    all_to_all x1, waiting for transfers between devices: 6.11 us -> 0.01 us  [on_device(): lax.all_to_all(chosen, 'freq', split_axis=0, concat_axis=0, tiled=True, a...]
    all_to_all x1, waiting for transfers between devices: 5.65 us -> 2.29 us  [on_device(): lax.all_to_all(packed.astype(jnp.float16), 'freq', split_axis=0, concat_a...]
    all_to_all x1, starting transfers between devices: 3.41 us -> 6.3 us  [on_device(): lax.all_to_all(chosen, 'freq', split_axis=0, concat_axis=0, tiled=True, a...]
    all_to_all x1, starting transfers between devices: 3.56 us -> 5.21 us  [on_device(): lax.all_to_all(packed.astype(jnp.float16), 'freq', split_axis=0, concat_a...]
    another operation x1, other arithmetic: 0.05 us -> 1 us  [on_device(): speed = jnp.stack([mine, swap_cores(mine, devices)])]
  transfers between devices with their start and end apart: 5 -> 4, of which waited for: 5 -> 3; matrix products, arithmetic and copies ran while one was open for 0% -> 0% of each run, Pallas kernels for 18% -> 19%
where the time goes in v3:
time: 61.4 us; the launch traced here: 60.9 us
  Pallas kernels  22.8 us (37%)
  blocking collectives  16.2 us (26%)
  starting transfers between devices  11.9 us (19%)
  waiting for transfers between devices  5.81 us (9%)
  other arithmetic  2.15 us (4%)
  local copies, waits for them, and re-layouts  0.98 us (2%)
  between operations  0.87 us (1%)
    all_to_all x1, blocking collectives, on_device(): lax.all_to_all(spectra.astype(jnp.float16), 'freq', split_axis=0, concat_...  16.2 us
    pallas_call x1, Pallas kernels, depth_steps(): pl.pallas_call(kernel, out_shape=(share, share, jax.ShapeDtypeStruct((2,...  7.52 us
    all_to_all x1, starting transfers between devices, on_device(): lax.all_to_all(chosen, 'freq', split_axis=0, concat_axis=0, tiled=True, a...  6.3 us
    all_to_all x1, starting transfers between devices, on_device(): lax.all_to_all(packed.astype(jnp.float16), 'freq', split_axis=0, concat_a...  5.21 us
    pallas_call x1, Pallas kernels, spectral_factors(): pl.pallas_call(factors_kernel, out_shape=pltpu.HBM((poly_coef.shape[2], 2...  4.41 us
    pallas_call x1, Pallas kernels, last_field(): pl.pallas_call(last_kernel, out_shape=jax.ShapeDtypeStruct((2, nx, ny), j...  4.16 us
    ppermute x2, waiting for transfers between devices, swap_cores(): return lax.ppermute(array, 'freq', [(i, i ^ 1) for i in range(count)])  3.52 us
    pallas_call x1, Pallas kernels, first_parts(): pl.pallas_call(first_kernel, out_shape=pltpu.VMEM((power_count, 2, nx, ny...  3.14 us
  transfers between devices with their start and end apart: 4, of which 3 were waited for; matrix products, arithmetic and copies ran while one was open for 0% of the time, Pallas kernels for 19%

profile of v3, /device:TPU:0, one launch (start us, length us, event | category | flops | bytes accessed | tf_op | source)
XLA Modules:
  0.0 60.9 jit_solution(11860023568091490248)
XLA Ops:
  0.6 0.0 copy-start.11
  0.7 2.7 %position_spectra.1 = f32[16,3,16,256]{3,2,1,0:T(8,128)S(1)} custom-call(s32[16]{0:T(128)} %refs_0_.1, bf16[32,256]{1,0:T(8,128)(2,1)} %constant.35.clone.table_hbm, bf16[16,256,256]{2,1,0:T(8,128)(2,1)} %traces_hbm.1, bf16[256,256]{1,0:T(8,128)(2,1)} %bitcast.25, bf16[256,256]{1,0:T(8,128)(2,1)} %constant.36.clone.rows_hbm, ...), custom_call_target="tpu_custom_call" | custom-call | flops 67108864 | bytes 2097152 | tf_op jit(solution)/shard_map/position_spectra/pallas_call | solution.py:430
  3.4 0.0 copy-start.9
  3.4 0.1 convert_element_type.23
  3.5 0.0 copy-start.3
  3.5 0.0 copy-start.7
  3.5 16.2 %all_to_all.15 = f16[16,3,16,256]{3,2,1,0:T(8,128)(2,1)S(1)} all-to-all(f16[16,3,16,256]{3,2,1,0:T(8,128)(2,1)S(1)} %convert_element_type.23), channel_id=1, replica_groups={{11,10,7,6,3,2,15,14,9,8,5,4,1,0,13,12},{27,26,23,22,19,18,31,30,25,24,..., dimensions={0} | all-to-all | bytes 786432 | tf_op jit(solution)/shard_map/all_to_all | solution.py:508
  19.8 0.2 convolution_convert_fusion
  20.0 0.7 %broadcast_in_dim.13 = bf16[8,4,16,256]{3,2,1,0:T(8,128)(2,1)} broadcast(bf16[4,16,256]{2,1,0:T(8,128)(2,1)S(1)} %bitcast.27), dimensions={1,2,3} | broadcast | bytes 294912 | tf_op jit(solution)/shard_map/broadcast_in_dim | solution.py:523
  20.7 6.3 %all-to-all-start.1 = ((bf16[8,4,16,256]{3,2,1,0:T(8,128)(2,1)}), bf16[8,4,16,256]{3,2,1,0:T(8,128)(2,1)}, u32[]{:S(2)}, u32[]{:S(2)}) async-start(bf16[8,4,16,256]{3,2,1,0:T(8,128)(2,1)} %broadcast_in_dim.13), calls=%async_computation.1 | async-start | bytes 524288 | tf_op jit(solution)/shard_map/all_to_all | solution.py:526
  27.1 0.0 copy-start.2
  27.1 0.0 copy-start.4
  27.1 0.1 copy.20.coef_ref
  27.2 0.1 multiply_bitcast_fusion
  27.3 4.4 %spectral_factors.1.factor_hbm.refs_4_ = f32[4,2,256,256]{3,2,1,0:T(8,128)} custom-call(f32[2,10,4]{2,1,0:T(8,128)S(1)} %copy.20.coef_ref, f32[256,1]{1,0:T(8,128)S(1)} %copy-done.3, f32[1,256]{1,0:T(1,128)S(1)} %copy-done.7), custom_call_target="tpu_custom_call" | custom-call | flops 10485760 | bytes 2097152 | tf_op jit(solution)/shard_map/spectral_factors/pallas_call | solution.py:169
  31.7 0.0 copy-done.1
  31.7 0.0 copy-start.8
  31.8 3.1 %first_parts.1.refs_5_ = f32[4,2,256,256]{3,2,1,0:T(8,128)S(1)} custom-call(bf16[4,256,256]{2,1,0:T(8,128)(2,1)S(1)} %copy-done.1, bf16[4,256,256]{2,1,0:T(8,128)(2,1)S(1)} %copy-done, bf16[256,256]{1,0:T(8,128)(2,1)S(1)} %copy-done.4, bf16[256,256]{1,0:T(8,128)(2,1)S(1)} %copy-done.2, f32[4,2,256,256]{3,2,1,0:T(8,128)} %spectral_factors.1.factor_hbm.refs_4_, ...), custom_call_target="tpu_custom_call" | custom-call | flops 1342177280 | bytes 4194304 | tf_op jit(solution)/shard_map/first_parts/pallas_call | solution.py:202
  34.9 0.0 all-to-all-done.1
  34.9 0.1 collective-permute-start
  35.1 1.7 %collective-permute-done = bf16[8,4,16,256]{3,2,1,0:T(8,128)(2,1)S(1)} collective-permute-done((bf16[8,4,16,256]{3,2,1,0:T(8,128)(2,1)}, bf16[8,4,16,256]{3,2,1,0:T(8,128)(2,1)S(1)}, u32[]{:S(2)}, u32[]{:S(2)}) %collective-permute-start) | collective-permute-done | bytes 262176 | tf_op jit(solution)/shard_map/ppermute | solution.py:494
  36.7 1.0 %pad_maximum_fusion.refs_6_ = bf16[2,8,4,16,256]{4,3,2,1,0:T(8,128)(2,1)S(1)} fusion(bf16[1,8,4,16,256]{4,3,2,1,0:T(8,128)(2,1)S(1)} %bitcast.24, bf16[1,8,4,16,256]{4,3,2,1,0:T(8,128)(2,1)} %bitcast.4), kind=kLoop, calls=%fused_computation.3 | loop fusion | flops 262144 | bytes 1048576 | tf_op jit(solution)/shard_map/stack | solution.py:535
  37.7 7.5 %depth_steps.1 = (f32[8,9,16,128]{3,2,1,0:T(8,128)S(1)}, f32[8,9,16,128]{3,2,1,0:T(8,128)S(1)}, f32[2,256,256]{2,1,0:T(8,128)S(1)}, f32[256,256]{1,0:T(8,128)S(1)}, f32[256,256]{1,0:T(8,128)S(1)}) custom-call(s32[16]{0:T(128)S(1)} %copy-done.8, s32[1]{0:T(128)} %bitcast.refs_1_.place_ref, bf16[4,256,256]{2,1,0:T(8,128)(2,1)} %constant.41.clone.left_ref.refs_2_.left_hbm, ...), custom_call_target="tpu_custom_call" | custom-call | flops 5368709120 | bytes 4194304 | tf_op jit(solution)/shard_map/depth_steps/pallas_call | solution.py:317
  45.3 0.2 collective-permute-start.1
  45.5 1.9 %collective-permute-done.1 = f32[8,9,16,128]{3,2,1,0:T(8,128)S(1)} collective-permute-done((f32[8,9,16,128]{3,2,1,0:T(8,128)S(1)}, f32[8,9,16,128]{3,2,1,0:T(8,128)S(1)}, u32[]{:S(2)}, u32[]{:S(2)}) %collective-permute-start.1) | collective-permute-done | bytes 589856 | tf_op jit(solution)/shard_map/ppermute | solution.py:494
  47.3 0.1 add.3
  47.5 0.1 fusion
  47.5 0.8 %pad_maximum_fusion.1 = f16[8,9,16,128]{3,2,1,0:T(8,128)(2,1)} fusion(f16[8,1,16,128]{3,2,1,0:T(8,128)(2,1)S(1)} %get-tuple-element.27, f16[8,8,16,128]{3,2,1,0:T(8,128)(2,1)S(1)} %fusion), kind=kLoop, calls=%fused_computation.5 | loop fusion | flops 147456 | bytes 589824 | tf_op jit(solution)/shard_map/concatenate | solution.py:542
  48.3 5.2 %all-to-all-start.2 = ((f16[8,9,16,128]{3,2,1,0:T(8,128)(2,1)}), f16[8,9,16,128]{3,2,1,0:T(8,128)(2,1)S(1)}, u32[]{:S(2)}, u32[]{:S(2)}) async-start(f16[8,9,16,128]{3,2,1,0:T(8,128)(2,1)} %pad_maximum_fusion.1), calls=%async_computation.2 | async-start | bytes 589824 | tf_op jit(solution)/shard_map/all_to_all | solution.py:543
  53.5 4.2 %last_field.1 = f32[2,256,256]{2,1,0:T(8,128)} custom-call(bf16[4,256,256]{2,1,0:T(8,128)(2,1)} %constant.41.clone.left_ref.refs_2_.left_hbm, bf16[4,256,256]{2,1,0:T(8,128)(2,1)} %constant.42.clone.right_ref.refs_3_.right_hbm, bf16[256,256]{1,0:T(8,128)(2,1)} %constant.37.clone.lanes_hbm.order_y_ref.order_x_hbm.order_y_hbm, ...), custom_call_target="tpu_custom_call" | custom-call | flops 671088640 | bytes 4194304 | tf_op jit(solution)/shard_map/last_field/pallas_call | solution.py:362
  57.7 2.3 %all-to-all-done.2 = f16[8,9,16,128]{3,2,1,0:T(8,128)(2,1)S(1)} async-done(((f16[8,9,16,128]{3,2,1,0:T(8,128)(2,1)}), f16[8,9,16,128]{3,2,1,0:T(8,128)(2,1)S(1)}, u32[]{:S(2)}, u32[]{:S(2)}) %all-to-all-start.2) | async-done | bytes 294944 | tf_op jit(solution)/shard_map/all_to_all | solution.py:543
  60.1 0.8 %image_rows.1 = f32[4,16,256]{2,1,0:T(8,128)} custom-call(s32[1]{0:T(128)} %bitcast.refs_1_.place_ref, f32[128,128]{1,0:T(8,128)S(1)} %copy-done.5, f32[64,64]{1,0:T(8,128)S(1)} %copy-done.6, f32[8,9,16,128]{3,2,1,0:T(8,128)S(1)} %convert_element_type.28.share_ref), custom_call_target="tpu_custom_call" | custom-call | tf_op jit(solution)/shard_map/image_rows/pallas_call | solution.py:483
  (22 shorter events, 0.2 us)
Async XLA Ops:
  0.6 19.1 %copy-start.10 = (s32[4]{0:T(128)S(1)}, s32[4]{0:T(128)}, u32[]{:S(2)}) copy-start(s32[4]{0:T(128)} %param.22) | copy-start | bytes 52
  0.6 19.1 %copy-start.11 = (s32[16]{0:T(128)S(1)}, s32[16]{0:T(128)}, u32[]{:S(2)}) copy-start(s32[16]{0:T(128)} %constant.40.clone) | copy-start | bytes 196
  3.4 23.7 %copy-start.9 = (f32[2,10,4]{1,2,0:T(4,128)S(1)}, f32[2,10,4]{1,2,0:T(4,128)}, u32[]{:S(2)}) copy-start(f32[2,10,4]{1,2,0:T(4,128)} %param.20) | copy-start | bytes 964
  3.5 23.8 %copy-start.3 = (f32[256,1]{1,0:T(8,128)S(1)}, f32[256,1]{1,0:T(8,128)}, u32[]{:S(2)}) copy-start(f32[256,1]{1,0:T(8,128)} %constant.38.clone.left_ref) | copy-start | bytes 3076
  3.5 23.8 %copy-start.7 = (f32[1,256]{1,0:T(1,128)S(1)}, f32[1,256]{1,0:T(1,128)}, u32[]{:S(2)}) copy-start(f32[1,256]{1,0:T(1,128)} %constant.39.clone.right_ref) | copy-start | bytes 3076
  20.7 14.2 %all-to-all-start.1 = ((bf16[8,4,16,256]{3,2,1,0:T(8,128)(2,1)}), bf16[8,4,16,256]{3,2,1,0:T(8,128)(2,1)}, u32[]{:S(2)}, u32[]{:S(2)}) async-start(bf16[8,4,16,256]{3,2,1,0:T(8,128)(2,1)} %broadcast_in_dim.13), calls=%async_computation.1 | async-start | bytes 524288 | tf_op jit(solution)/shard_map/all_to_all | solution.py:526
  27.0 4.7 %copy-start = (bf16[4,256,256]{2,1,0:T(8,128)(2,1)S(1)}, bf16[4,256,256]{2,1,0:T(8,128)(2,1)}, u32[]{:S(2)}) copy-start(bf16[4,256,256]{2,1,0:T(8,128)(2,1)} %constant.42.clone.right_ref.refs_3_.right_hbm) | copy-start | bytes 1572868
  27.0 4.7 %copy-start.1 = (bf16[4,256,256]{2,1,0:T(8,128)(2,1)S(1)}, bf16[4,256,256]{2,1,0:T(8,128)(2,1)}, u32[]{:S(2)}) copy-start(bf16[4,256,256]{2,1,0:T(8,128)(2,1)} %constant.41.clone.left_ref.refs_2_.left_hbm) | copy-start | bytes 1572868
  27.1 4.7 %copy-start.2 = (bf16[256,256]{1,0:T(8,128)(2,1)S(1)}, bf16[256,256]{1,0:T(8,128)(2,1)}, u32[]{:S(2)}) copy-start(bf16[256,256]{1,0:T(8,128)(2,1)} %constant.37.clone.lanes_hbm.order_y_ref.order_x_hbm.order_y_hbm) | copy-start | bytes 393220
  27.1 4.7 %copy-start.4 = (bf16[256,256]{1,0:T(8,128)(2,1)S(1)}, bf16[256,256]{1,0:T(8,128)(2,1)}, u32[]{:S(2)}) copy-start(bf16[256,256]{1,0:T(8,128)(2,1)} %constant.43.clone.order_x_ref) | copy-start | bytes 393220
  31.7 6.0 %copy-start.8 = (s32[16]{0:T(128)S(1)}, s32[16]{0:T(128)}, u32[]{:S(2)}) copy-start(s32[16]{0:T(128)} %refs_0_.1) | copy-start | bytes 196
  34.9 1.8 %collective-permute-start = (bf16[8,4,16,256]{3,2,1,0:T(8,128)(2,1)}, bf16[8,4,16,256]{3,2,1,0:T(8,128)(2,1)S(1)}, u32[]{:S(2)}, u32[]{:S(2)}) collective-permute-start(bf16[8,4,16,256]{3,2,1,0:T(8,128)(2,1)} %all-to-all-done.1), channel_id=1, source_target_pairs={{0,1},{1,0},{2,3},{3,2},{4,5},{5,4},{6,7},{7,6},{8,9},{9,8},{10,11... | collective-permute-start | bytes 786440 | tf_op jit(solution)/shard_map/ppermute | solution.py:494
  45.3 2.1 %collective-permute-start.1 = (f32[8,9,16,128]{3,2,1,0:T(8,128)S(1)}, f32[8,9,16,128]{3,2,1,0:T(8,128)S(1)}, u32[]{:S(2)}, u32[]{:S(2)}) collective-permute-start(f32[8,9,16,128]{3,2,1,0:T(8,128)S(1)} %get-tuple-element.18), channel_id=1, source_target_pairs={{0,1},{1,0},{2,3},{3,2},{4,5},{5,4},{6,7},{7,6},{8,9},{9,8},{10,11... | collective-permute-start | bytes 1769480 | tf_op jit(solution)/shard_map/ppermute | solution.py:494
  48.3 11.7 %all-to-all-start.2 = ((f16[8,9,16,128]{3,2,1,0:T(8,128)(2,1)}), f16[8,9,16,128]{3,2,1,0:T(8,128)(2,1)S(1)}, u32[]{:S(2)}, u32[]{:S(2)}) async-start(f16[8,9,16,128]{3,2,1,0:T(8,128)(2,1)} %pad_maximum_fusion.1), calls=%async_computation.2 | async-start | bytes 589824 | tf_op jit(solution)/shard_map/all_to_all | solution.py:543
  53.5 6.5 %copy-start.5 = (f32[128,128]{1,0:T(8,128)S(1)}, f32[128,128]{1,0:T(8,128)}, u32[]{:S(2)}) copy-start(f32[128,128]{1,0:T(8,128)} %constant.44.clone.lanes_ref) | copy-start | bytes 196612
  53.5 6.5 %copy-start.6 = (f32[64,64]{1,0:T(8,128)S(1)}, f32[64,64]{1,0:T(8,128)}, u32[]{:S(2)}) copy-start(f32[64,64]{1,0:T(8,128)} %constant.45.clone.rows_ref) | copy-start | bytes 49156

commit v4 on v3

--- a/solution.py
+++ b/solution.py
@@ -142,13 +142,13 @@
                 state[c, rows, lanes] = total
 
 
-def factors_kernel(coef_ref, left_ref, right_ref, out_ref):
+def store_factors(coef_ref, lambda_x_ref, lambda_y_ref, factor_ref):
     term_count, power_count = coef_ref.shape[1:]
     block = 32
 
     def rows_step(i, carry):
         rows = pl.ds(pl.multiple_of(i * block, block), block)
-        g = left_ref[rows, :] * right_ref[0:1, :] * 0.125 - 1.0
+        g = lambda_x_ref[rows, :] * lambda_y_ref[0:1, :] * 0.125 - 1.0
         twice = 2.0 * g
         sums = [[coef_ref[c, 0, j] + coef_ref[c, 1, j] * g for c in range(2)] for j in range(power_count)]
         before, now = jnp.ones_like(g), g
@@ -159,63 +159,73 @@
                     sums[j][c] = sums[j][c] + coef_ref[c, k, j] * now
         for j in range(power_count):
             for c in range(2):
-                out_ref[j, c, rows, :] = sums[j][c]
+                factor_ref[j, c, rows, :] = sums[j][c]
         return carry
 
-    lax.fori_loop(0, left_ref.shape[0] // block, rows_step, 0)
-
-
-def spectral_factors(poly_coef, nx, ny):
+    lax.fori_loop(0, lambda_x_ref.shape[0] // block, rows_step, 0)
+
+
+def first_kernel(
+    coef_ref, lambda_x_ref, lambda_y_ref, left_hbm, right_hbm, order_x_hbm, order_y_hbm, start_ref,
+    part_ref, factor_hbm, spectrum, columns, factor_ref, left_ref, right_ref, order_x_ref, order_y_ref, sems,
+    *, arrival,
+):
+    rows = start_ref.shape[1] // len(arrival)
+    pairs = [
+        (left_hbm, left_ref), (right_hbm, right_ref), (order_x_hbm, order_x_ref), (order_y_hbm, order_y_ref),
+        (factor_ref, factor_hbm),
+    ]
+    *fetches, put = [
+        pltpu.make_async_copy(source, target, sems.at[i]) for i, (source, target) in enumerate(pairs)
+    ]
+    for fetch in fetches:
+        fetch.start()
+    store_factors(coef_ref, lambda_x_ref, lambda_y_ref, factor_ref)
+    put.start()
+    for fetch in fetches:
+        fetch.wait()
+    for c in range(2):
+        natural = jnp.concatenate([start_ref[c, i * rows : (i + 1) * rows] for i in arrival], axis=0)
+        spectrum[c] = forward(reorder(natural, order_x_ref[...], order_y_ref[...]), left_ref, right_ref)
+    half_parts(left_ref, factor_ref, spectrum, columns, range(2))
+    for j in range(part_ref.shape[0]):
+        for c in range(2):
+            part_ref[j, c] = inverse_y(columns[j, c], right_ref)
+    put.wait()
+
+
+def first_parts(poly_coef, left, right, order_x, order_y, start, arrival):
+    _, nx, ny = start.shape
+    shape = (poly_coef.shape[2], 2, nx, ny)
+    tables = [left, right, order_x, order_y]
+
+    def kernel(*refs):
+        first_kernel(*refs, arrival=arrival)
+
     return pl.pallas_call(
-        factors_kernel,
-        out_shape=pltpu.HBM((poly_coef.shape[2], 2, nx, ny), jnp.float32),
-        in_specs=[SMEM, VMEM, VMEM],
-        out_specs=VMEM,
-        compiler_params=pltpu.CompilerParams(vmem_limit_bytes=6 * 1024 * 1024),
+        kernel,
+        out_shape=(pltpu.VMEM(shape, jnp.float32), pltpu.HBM(shape, jnp.float32)),
+        in_specs=[SMEM, VMEM, VMEM, HBM, HBM, HBM, HBM, VMEM],
+        out_specs=(VMEM, HBM),
+        scratch_shapes=[
+            pltpu.VMEM((2, nx, ny), jnp.float32),
+            pltpu.VMEM(shape, jnp.float32),
+            pltpu.VMEM(shape, jnp.float32),
+            *(pltpu.VMEM(table.shape, table.dtype) for table in tables),
+            pltpu.SemaphoreType.DMA((5,)),
+        ],
+        compiler_params=pltpu.CompilerParams(vmem_limit_bytes=12 * 1024 * 1024),
         cost_estimate=pl.CostEstimate(
-            flops=poly_coef.size * 2 * nx * ny, bytes_accessed=32 * nx * ny, transcendentals=0
+            flops=80 * nx * ny * (nx + ny) // 2, bytes_accessed=64 * nx * ny, transcendentals=0
         ),
-        name="spectral_factors",
+        name="first_parts",
     )(
         poly_coef,
         jnp.asarray(eigenvalues(nx)[:, None], jnp.float32),
         jnp.asarray(eigenvalues(ny)[None, :], jnp.float32),
-    )
-
-
-def first_kernel(
-    left_ref, right_ref, order_x_ref, order_y_ref, factor_hbm, start_ref, part_ref, spectrum, columns, factor_ref, sem
-):
-    fetch = pltpu.make_async_copy(factor_hbm, factor_ref, sem)
-    fetch.start()
-    for c in range(2):
-        spectrum[c] = forward(reorder(start_ref[c], order_x_ref[...], order_y_ref[...]), left_ref, right_ref)
-    fetch.wait()
-    half_parts(left_ref, factor_ref, spectrum, columns, range(2))
-    for j in range(part_ref.shape[0]):
-        for c in range(2):
-            part_ref[j, c] = inverse_y(columns[j, c], right_ref)
-
-
-def first_parts(left, right, order_x, order_y, factors, start):
-    power_count, _, nx, ny = factors.shape
-    return pl.pallas_call(
-        first_kernel,
-        out_shape=pltpu.VMEM((power_count, 2, nx, ny), jnp.float32),
-        in_specs=[VMEM, VMEM, VMEM, VMEM, HBM, VMEM],
-        out_specs=VMEM,
-        scratch_shapes=[
-            pltpu.VMEM((2, nx, ny), jnp.float32),
-            pltpu.VMEM(factors.shape, jnp.float32),
-            pltpu.VMEM(factors.shape, jnp.float32),
-            pltpu.SemaphoreType.DMA,
-        ],
-        compiler_params=pltpu.CompilerParams(vmem_limit_bytes=10 * 1024 * 1024),
-        cost_estimate=pl.CostEstimate(
-            flops=80 * nx * ny * (nx + ny) // 2, bytes_accessed=64 * nx * ny, transcendentals=0
-        ),
-        name="first_parts",
-    )(left, right, order_x, order_y, in_hbm(factors), start)
+        *(in_hbm(table) for table in tables),
+        start,
+    )
 
 
 def depth_kernel(
@@ -513,8 +523,6 @@
         tiled=True,
         axis_index_groups=[order],
     )
-    received, poly_coef = lax.optimization_barrier((received, poly_coef))
-    factors = spectral_factors(poly_coef, nx, ny)
     start = received[:, :2].transpose(1, 0, 2, 3).reshape(2, nx, ny).astype(jnp.float32) / SPECTRA_SCALE
 
     owned = (depth_owner[:, None] == jnp.asarray(order, jnp.int32)[None, :]).astype(jnp.bfloat16)
@@ -529,8 +537,8 @@
     left = jnp.asarray(np.swapaxes(right_matrices(nx), 1, 2))
     right = jnp.asarray(right_matrices(ny))
     order_x, order_y = jnp.asarray(fold_matrix(nx)), jnp.asarray(fold_matrix(ny))
-    arrived = (np.array(order)[:, None] * local_x + np.arange(local_x)).reshape(-1)
-    parts = first_parts(left, right, jnp.asarray(fold_matrix(nx)[:, arrived]), order_y, factors, start)
+    arrival = [order.index(i) for i in range(devices)]
+    parts, factors = first_parts(poly_coef, left, right, order_x, order_y, start, arrival)
     parts, mine = lax.optimization_barrier((parts, mine))
     speed = jnp.stack([mine, swap_cores(mine, devices)])
     keep, send, spectrum, real, slow = depth_steps(

time: 61.4 us -> 59.4 us (0.967)
  Pallas kernels: 22.8 us -> 21.5 us
  other arithmetic: 2.15 us -> 1.21 us
    pallas_call x2 -> x1, Pallas kernels: 7.56 us -> 6.27 us  [first_parts(): pl.pallas_call(kernel, out_shape=(pltpu.VMEM(shape, jnp.float32), pltpu.H...]
    all_to_all x1, starting transfers between devices: 5.21 us -> 6.43 us  [on_device(): lax.all_to_all(packed.astype(jnp.float16), 'freq', split_axis=0, concat_a...]
    another operation x1, other arithmetic: 1 us -> 0.05 us  [on_device(): speed = jnp.stack([mine, swap_cores(mine, devices)])]
  transfers between devices with their start and end apart: 4 -> 4, of which waited for: 3 -> 3; matrix products, arithmetic and copies ran while one was open for 0% -> 0% of each run, Pallas kernels for 19% -> 18%
where the time goes in v4:
time: 59.4 us; the launch traced here: 59 us
  Pallas kernels  21.5 us (36%)
  blocking collectives  16.2 us (27%)
  starting transfers between devices  12.5 us (21%)
  waiting for transfers between devices  5.63 us (9%)
  other arithmetic  1.21 us (2%)
  local copies, waits for them, and re-layouts  0.96 us (2%)
  between operations  0.84 us (1%)
    all_to_all x1, blocking collectives, on_device(): lax.all_to_all(spectra.astype(jnp.float16), 'freq', split_axis=0, concat_...  16.2 us
    pallas_call x1, Pallas kernels, depth_steps(): pl.pallas_call(kernel, out_shape=(share, share, jax.ShapeDtypeStruct((2,...  7.54 us
    all_to_all x1, starting transfers between devices, on_device(): lax.all_to_all(packed.astype(jnp.float16), 'freq', split_axis=0, concat_a...  6.43 us
    pallas_call x1, Pallas kernels, first_parts(): pl.pallas_call(kernel, out_shape=(pltpu.VMEM(shape, jnp.float32), pltpu.H...  6.27 us
    all_to_all x1, starting transfers between devices, on_device(): lax.all_to_all(chosen, 'freq', split_axis=0, concat_axis=0, tiled=True, a...  5.69 us
    pallas_call x1, Pallas kernels, last_field(): pl.pallas_call(last_kernel, out_shape=jax.ShapeDtypeStruct((2, nx, ny), j...  4.16 us
    ppermute x2, waiting for transfers between devices, swap_cores(): return lax.ppermute(array, 'freq', [(i, i ^ 1) for i in range(count)])  3.34 us
    pallas_call x1, Pallas kernels, position_spectra(): pl.pallas_call(spectra_kernel, out_shape=jax.ShapeDtypeStruct((slots, 3,...  2.7 us
  transfers between devices with their start and end apart: 4, of which 3 were waited for; matrix products, arithmetic and copies ran while one was open for 0% of the time, Pallas kernels for 18%

profile of v4, /device:TPU:0, one launch (start us, length us, event | category | flops | bytes accessed | tf_op | source)
XLA Modules:
  0.0 59.0 jit_solution(16753976650350921613)
XLA Ops:
  0.6 0.0 copy-start.6
  0.6 0.0 copy-start.7
  0.7 2.7 %position_spectra.1 = f32[16,3,16,256]{3,2,1,0:T(8,128)S(1)} custom-call(s32[16]{0:T(128)} %refs_0_.2, bf16[32,256]{1,0:T(8,128)(2,1)} %constant.33.clone.table_hbm, bf16[16,256,256]{2,1,0:T(8,128)(2,1)} %traces_hbm.1, bf16[256,256]{1,0:T(8,128)(2,1)} %bitcast.26, bf16[256,256]{1,0:T(8,128)(2,1)} %constant.34.clone.rows_hbm, ...), custom_call_target="tpu_custom_call" | custom-call | flops 67108864 | bytes 2097152 | tf_op jit(solution)/shard_map/position_spectra/pallas_call | solution.py:440
  3.4 0.0 copy-start.5
  3.4 0.1 convert_element_type.23
  3.5 0.0 copy-start.3
  3.5 0.0 copy-start.4
  3.5 16.2 %all_to_all.15 = f16[16,3,16,256]{3,2,1,0:T(8,128)(2,1)S(1)} all-to-all(f16[16,3,16,256]{3,2,1,0:T(8,128)(2,1)S(1)} %convert_element_type.23), channel_id=1, replica_groups={{11,10,7,6,3,2,15,14,9,8,5,4,1,0,13,12},{27,26,23,22,19,18,31,30,25,24,..., dimensions={0} | all-to-all | bytes 786432 | tf_op jit(solution)/shard_map/all_to_all | solution.py:518
  19.8 0.0 copy-done.6
  19.8 0.0 copy-done.7
  19.8 0.2 convolution_convert_fusion
  20.0 0.7 %broadcast_in_dim.13 = bf16[8,4,16,256]{3,2,1,0:T(8,128)(2,1)} broadcast(bf16[4,16,256]{2,1,0:T(8,128)(2,1)S(1)} %bitcast.28), dimensions={1,2,3} | broadcast | bytes 294912 | tf_op jit(solution)/shard_map/broadcast_in_dim | solution.py:531
  20.7 5.7 %all-to-all-start.1 = ((bf16[8,4,16,256]{3,2,1,0:T(8,128)(2,1)}), bf16[8,4,16,256]{3,2,1,0:T(8,128)(2,1)S(1)}, u32[]{:S(2)}, u32[]{:S(2)}) async-start(bf16[8,4,16,256]{3,2,1,0:T(8,128)(2,1)} %broadcast_in_dim.13), calls=%async_computation.1 | async-start | bytes 524288 | tf_op jit(solution)/shard_map/all_to_all | solution.py:534
  26.4 0.0 copy-done.5
  26.4 0.1 copy.20.refs_0_
  26.5 0.1 multiply_bitcast_fusion
  26.7 0.0 copy-start.2
  26.7 6.3 %first_parts.1 = (f32[4,2,256,256]{3,2,1,0:T(8,128)S(1)}, f32[4,2,256,256]{3,2,1,0:T(8,128)}) custom-call(f32[2,10,4]{2,1,0:T(8,128)S(1)} %copy.20.refs_0_, f32[256,1]{1,0:T(8,128)S(1)} %copy-done.3, f32[1,256]{1,0:T(1,128)S(1)} %copy-done.4, bf16[4,256,256]{2,1,0:T(8,128)(2,1)} %constant.37.clone.refs_3_.refs_2_.left_hbm, ...), custom_call_target="tpu_custom_call" | custom-call | flops 1342177280 | bytes 4194304 | tf_op jit(solution)/shard_map/first_parts/pallas_call | solution.py:205
  33.0 0.0 all-to-all-done.1
  33.0 0.1 collective-permute-start
  33.1 1.5 %collective-permute-done = bf16[8,4,16,256]{3,2,1,0:T(8,128)(2,1)S(1)} collective-permute-done((bf16[8,4,16,256]{3,2,1,0:T(8,128)(2,1)S(1)}, bf16[8,4,16,256]{3,2,1,0:T(8,128)(2,1)S(1)}, u32[]{:S(2)}, u32[]{:S(2)}) %collective-permute-start) | collective-permute-done | bytes 262176 | tf_op jit(solution)/shard_map/ppermute | solution.py:504
  34.6 0.1 pad_maximum_fusion.refs_6_
  34.6 7.5 %depth_steps.1 = (f32[8,9,16,128]{3,2,1,0:T(8,128)S(1)}, f32[8,9,16,128]{3,2,1,0:T(8,128)S(1)}, f32[2,256,256]{2,1,0:T(8,128)S(1)}, f32[256,256]{1,0:T(8,128)S(1)}, f32[256,256]{1,0:T(8,128)S(1)}) custom-call(s32[16]{0:T(128)S(1)} %copy-done.2, s32[1]{0:T(128)} %bitcast.refs_1_.place_ref, bf16[4,256,256]{2,1,0:T(8,128)(2,1)} %constant.37.clone.refs_3_.refs_2_.left_hbm, ...), custom_call_target="tpu_custom_call" | custom-call | flops 5368709120 | bytes 4194304 | tf_op jit(solution)/shard_map/depth_steps/pallas_call | solution.py:327
  42.2 0.2 collective-permute-start.1
  42.4 1.9 %collective-permute-done.1 = f32[8,9,16,128]{3,2,1,0:T(8,128)S(1)} collective-permute-done((f32[8,9,16,128]{3,2,1,0:T(8,128)S(1)}, f32[8,9,16,128]{3,2,1,0:T(8,128)S(1)}, u32[]{:S(2)}, u32[]{:S(2)}) %collective-permute-start.1) | collective-permute-done | bytes 589856 | tf_op jit(solution)/shard_map/ppermute | solution.py:504
  44.3 0.1 add.3
  44.4 0.1 fusion
  44.4 0.8 %pad_maximum_fusion.1 = f16[8,9,16,128]{3,2,1,0:T(8,128)(2,1)} fusion(f16[8,1,16,128]{3,2,1,0:T(8,128)(2,1)S(1)} %get-tuple-element.27, f16[8,8,16,128]{3,2,1,0:T(8,128)(2,1)S(1)} %fusion), kind=kLoop, calls=%fused_computation.5 | loop fusion | flops 147456 | bytes 589824 | tf_op jit(solution)/shard_map/concatenate | solution.py:550
  45.2 6.4 %all-to-all-start.2 = ((f16[8,9,16,128]{3,2,1,0:T(8,128)(2,1)}), f16[8,9,16,128]{3,2,1,0:T(8,128)(2,1)S(1)}, u32[]{:S(2)}, u32[]{:S(2)}) async-start(f16[8,9,16,128]{3,2,1,0:T(8,128)(2,1)} %pad_maximum_fusion.1), calls=%async_computation.2 | async-start | bytes 589824 | tf_op jit(solution)/shard_map/all_to_all | solution.py:551
  51.7 4.2 %last_field.1 = f32[2,256,256]{2,1,0:T(8,128)} custom-call(bf16[4,256,256]{2,1,0:T(8,128)(2,1)} %constant.37.clone.refs_3_.refs_2_.left_hbm, bf16[4,256,256]{2,1,0:T(8,128)(2,1)} %constant.38.clone.refs_4_.refs_3_.right_hbm, bf16[256,256]{1,0:T(8,128)(2,1)} %constant.35.clone.lanes_hbm.refs_5_.refs_6_.order_x_hbm.order_y_hbm, ...), custom_call_target="tpu_custom_call" | custom-call | flops 671088640 | bytes 4194304 | tf_op jit(solution)/shard_map/last_field/pallas_call | solution.py:372
  55.8 2.3 %all-to-all-done.2 = f16[8,9,16,128]{3,2,1,0:T(8,128)(2,1)S(1)} async-done(((f16[8,9,16,128]{3,2,1,0:T(8,128)(2,1)}), f16[8,9,16,128]{3,2,1,0:T(8,128)(2,1)S(1)}, u32[]{:S(2)}, u32[]{:S(2)}) %all-to-all-start.2) | async-done | bytes 294944 | tf_op jit(solution)/shard_map/all_to_all | solution.py:551
  58.2 0.8 %image_rows.1 = f32[4,16,256]{2,1,0:T(8,128)} custom-call(s32[1]{0:T(128)} %bitcast.refs_1_.place_ref, f32[128,128]{1,0:T(8,128)S(1)} %copy-done, f32[64,64]{1,0:T(8,128)S(1)} %copy-done.1, f32[8,9,16,128]{3,2,1,0:T(8,128)S(1)} %convert_element_type.28.share_ref), custom_call_target="tpu_custom_call" | custom-call | tf_op jit(solution)/shard_map/image_rows/pallas_call | solution.py:493
  (13 shorter events, 0.2 us)
Async XLA Ops:
  0.6 19.1 %copy-start.6 = (s32[4]{0:T(128)S(1)}, s32[4]{0:T(128)}, u32[]{:S(2)}) copy-start(s32[4]{0:T(128)} %param.21) | copy-start | bytes 52
  0.6 19.1 %copy-start.7 = (s32[16]{0:T(128)S(1)}, s32[16]{0:T(128)}, u32[]{:S(2)}) copy-start(s32[16]{0:T(128)} %constant.36.clone) | copy-start | bytes 196
  3.4 23.1 %copy-start.5 = (f32[2,10,4]{1,2,0:T(4,128)S(1)}, f32[2,10,4]{1,2,0:T(4,128)}, u32[]{:S(2)}) copy-start(f32[2,10,4]{1,2,0:T(4,128)} %param.19) | copy-start | bytes 964
  3.5 23.2 %copy-start.3 = (f32[256,1]{1,0:T(8,128)S(1)}, f32[256,1]{1,0:T(8,128)}, u32[]{:S(2)}) copy-start(f32[256,1]{1,0:T(8,128)} %constant.39.clone.refs_1_) | copy-start | bytes 3076
  3.5 23.2 %copy-start.4 = (f32[1,256]{1,0:T(1,128)S(1)}, f32[1,256]{1,0:T(1,128)}, u32[]{:S(2)}) copy-start(f32[1,256]{1,0:T(1,128)} %constant.40.clone.refs_2_) | copy-start | bytes 3076
  20.7 12.2 %all-to-all-start.1 = ((bf16[8,4,16,256]{3,2,1,0:T(8,128)(2,1)}), bf16[8,4,16,256]{3,2,1,0:T(8,128)(2,1)S(1)}, u32[]{:S(2)}, u32[]{:S(2)}) async-start(bf16[8,4,16,256]{3,2,1,0:T(8,128)(2,1)} %broadcast_in_dim.13), calls=%async_computation.1 | async-start | bytes 524288 | tf_op jit(solution)/shard_map/all_to_all | solution.py:534
  26.7 8.0 %copy-start.2 = (s32[16]{0:T(128)S(1)}, s32[16]{0:T(128)}, u32[]{:S(2)}) copy-start(s32[16]{0:T(128)} %refs_0_.2) | copy-start | bytes 196
  33.0 1.6 %collective-permute-start = (bf16[8,4,16,256]{3,2,1,0:T(8,128)(2,1)S(1)}, bf16[8,4,16,256]{3,2,1,0:T(8,128)(2,1)S(1)}, u32[]{:S(2)}, u32[]{:S(2)}) collective-permute-start(bf16[8,4,16,256]{3,2,1,0:T(8,128)(2,1)S(1)} %all-to-all-done.1), channel_id=1, source_target_pairs={{0,1},{1,0},{2,3},{3,2},{4,5},{5,4},{6,7},{7,6},{8,9},{9,8},{10,11... | collective-permute-start | bytes 786440 | tf_op jit(solution)/shard_map/ppermute | solution.py:504
  42.2 2.1 %collective-permute-start.1 = (f32[8,9,16,128]{3,2,1,0:T(8,128)S(1)}, f32[8,9,16,128]{3,2,1,0:T(8,128)S(1)}, u32[]{:S(2)}, u32[]{:S(2)}) collective-permute-start(f32[8,9,16,128]{3,2,1,0:T(8,128)S(1)} %get-tuple-element.18), channel_id=1, source_target_pairs={{0,1},{1,0},{2,3},{3,2},{4,5},{5,4},{6,7},{7,6},{8,9},{9,8},{10,11... | collective-permute-start | bytes 1769480 | tf_op jit(solution)/shard_map/ppermute | solution.py:504
  45.2 12.9 %all-to-all-start.2 = ((f16[8,9,16,128]{3,2,1,0:T(8,128)(2,1)}), f16[8,9,16,128]{3,2,1,0:T(8,128)(2,1)S(1)}, u32[]{:S(2)}, u32[]{:S(2)}) async-start(f16[8,9,16,128]{3,2,1,0:T(8,128)(2,1)} %pad_maximum_fusion.1), calls=%async_computation.2 | async-start | bytes 589824 | tf_op jit(solution)/shard_map/all_to_all | solution.py:551
  51.7 6.5 %copy-start = (f32[128,128]{1,0:T(8,128)S(1)}, f32[128,128]{1,0:T(8,128)}, u32[]{:S(2)}) copy-start(f32[128,128]{1,0:T(8,128)} %constant.41.clone.lanes_ref) | copy-start | bytes 196612
  51.7 6.5 %copy-start.1 = (f32[64,64]{1,0:T(8,128)S(1)}, f32[64,64]{1,0:T(8,128)}, u32[]{:S(2)}) copy-start(f32[64,64]{1,0:T(8,128)} %constant.42.clone.rows_ref) | copy-start | bytes 49156

commit v5 on v4

--- a/solution.py
+++ b/solution.py
@@ -20,7 +20,7 @@
 def device_order(devices):
     length = devices // 4
     along = list(range(length // 2, -1, -1)) + list(range(length // 2 + 1, length))
-    return [4 * z + 2 * y + core for y in (1, 0) for z in along for core in (1, 0)]
+    return [4 * z + 2 * y + core for core in (1, 0) for z in along for y in (1, 0)]
 
 
 def chip_order(chips):
@@ -393,7 +393,7 @@
     out_ref, slot_ref, table_ref, traces_ref, speed_ref, rows_ref, lanes_ref, bins, sems,
 ):
     slots, _, local_x, ny = out_ref.shape
-    chunk = max(local_x // 4, 1)
+    chunk = max(local_x // 2, 1)
     pairs = [
         (table_hbm, table_ref), (slot_hbm, slot_ref), (speed_hbm, speed_ref), (lanes_hbm, lanes_ref),
         (rows_hbm, rows_ref),
@@ -436,7 +436,7 @@
     order[order.shape[0] // 2 :] = order[order.shape[0] // 2 :, ::-1]
     rows = jnp.asarray(np.eye(nx)[order.reshape(-1)].astype(jnp.bfloat16))
     lanes = jnp.asarray(fold_matrix(ny))
-    chunk = max(local_x // 4, 1)
+    chunk = max(local_x // 2, 1)
     return pl.pallas_call(
         spectra_kernel,
         out_shape=jax.ShapeDtypeStruct((slots, 3, local_x, ny), jnp.float32),

time: 59.4 us -> 58.9 us (level)
  starting transfers between devices: 12.5 us -> 11.9 us
    all_to_all x1, starting transfers between devices: 6.43 us -> 5.62 us  [on_device(): lax.all_to_all(packed.astype(jnp.float16), 'freq', split_axis=0, concat_a...]
where the time goes in v5:
time: 58.9 us; the launch traced here: 58.5 us
  Pallas kernels  21.3 us (36%)
  blocking collectives  16.4 us (28%)
  starting transfers between devices  11.9 us (20%)
  waiting for transfers between devices  5.69 us (10%)
  other arithmetic  1.21 us (2%)
  local copies, waits for them, and re-layouts  0.96 us (2%)
  between operations  0.85 us (1%)
    all_to_all x1, blocking collectives, on_device(): lax.all_to_all(spectra.astype(jnp.float16), 'freq', split_axis=0, concat_...  16.4 us
    pallas_call x1, Pallas kernels, depth_steps(): pl.pallas_call(kernel, out_shape=(share, share, jax.ShapeDtypeStruct((2,...  7.54 us
    pallas_call x1, Pallas kernels, first_parts(): pl.pallas_call(kernel, out_shape=(pltpu.VMEM(shape, jnp.float32), pltpu.H...  6.27 us
    all_to_all x1, starting transfers between devices, on_device(): lax.all_to_all(chosen, 'freq', split_axis=0, concat_axis=0, tiled=True, a...  6.01 us
    all_to_all x1, starting transfers between devices, on_device(): lax.all_to_all(packed.astype(jnp.float16), 'freq', split_axis=0, concat_a...  5.62 us
    pallas_call x1, Pallas kernels, last_field(): pl.pallas_call(last_kernel, out_shape=jax.ShapeDtypeStruct((2, nx, ny), j...  4.16 us
    ppermute x2, waiting for transfers between devices, swap_cores(): return lax.ppermute(array, 'freq', [(i, i ^ 1) for i in range(count)])  3.4 us
    pallas_call x1, Pallas kernels, position_spectra(): pl.pallas_call(spectra_kernel, out_shape=jax.ShapeDtypeStruct((slots, 3,...  2.44 us
  transfers between devices with their start and end apart: 4, of which 3 were waited for; matrix products, arithmetic and copies ran while one was open for 0% of the time, Pallas kernels for 18%

profile of v5, /device:TPU:0, one launch (start us, length us, event | category | flops | bytes accessed | tf_op | source)
XLA Modules:
  0.0 58.5 jit_solution(13537298668394564967)
XLA Ops:
  0.6 0.0 copy-start.6
  0.6 0.0 copy-start.7
  0.7 2.4 %position_spectra.1 = f32[16,3,16,256]{3,2,1,0:T(8,128)S(1)} custom-call(s32[16]{0:T(128)} %refs_0_.2, bf16[32,256]{1,0:T(8,128)(2,1)} %constant.33.clone.table_hbm, bf16[16,256,256]{2,1,0:T(8,128)(2,1)} %traces_hbm.1, bf16[256,256]{1,0:T(8,128)(2,1)} %bitcast.26, bf16[256,256]{1,0:T(8,128)(2,1)} %constant.34.clone.rows_hbm, ...), custom_call_target="tpu_custom_call" | custom-call | flops 67108864 | bytes 2097152 | tf_op jit(solution)/shard_map/position_spectra/pallas_call | solution.py:440
  3.1 0.0 copy-start.5
  3.1 0.1 convert_element_type.23
  3.2 0.0 copy-start.3
  3.2 0.0 copy-start.4
  3.2 16.4 %all_to_all.15 = f16[16,3,16,256]{3,2,1,0:T(8,128)(2,1)S(1)} all-to-all(f16[16,3,16,256]{3,2,1,0:T(8,128)(2,1)S(1)} %convert_element_type.23), channel_id=1, replica_groups={{11,9,7,5,3,1,15,13,10,8,6,4,2,0,14,12},{27,25,23,21,19,17,31,29,26,24,..., dimensions={0} | all-to-all | bytes 786432 | tf_op jit(solution)/shard_map/all_to_all | solution.py:518
  19.7 0.0 copy-done.6
  19.7 0.0 copy-done.7
  19.7 0.2 convolution_convert_fusion
  20.0 0.7 %broadcast_in_dim.13 = bf16[8,4,16,256]{3,2,1,0:T(8,128)(2,1)} broadcast(bf16[4,16,256]{2,1,0:T(8,128)(2,1)S(1)} %bitcast.28), dimensions={1,2,3} | broadcast | bytes 294912 | tf_op jit(solution)/shard_map/broadcast_in_dim | solution.py:531
  20.7 6.0 %all-to-all-start.1 = ((bf16[8,4,16,256]{3,2,1,0:T(8,128)(2,1)}), bf16[8,4,16,256]{3,2,1,0:T(8,128)(2,1)S(1)}, u32[]{:S(2)}, u32[]{:S(2)}) async-start(bf16[8,4,16,256]{3,2,1,0:T(8,128)(2,1)} %broadcast_in_dim.13), calls=%async_computation.1 | async-start | bytes 524288 | tf_op jit(solution)/shard_map/all_to_all | solution.py:534
  26.7 0.0 copy-done.5
  26.7 0.1 copy.20.refs_0_
  26.8 0.1 multiply_bitcast_fusion
  26.9 0.0 copy-start.2
  27.0 6.3 %first_parts.1 = (f32[4,2,256,256]{3,2,1,0:T(8,128)S(1)}, f32[4,2,256,256]{3,2,1,0:T(8,128)}) custom-call(f32[2,10,4]{2,1,0:T(8,128)S(1)} %copy.20.refs_0_, f32[256,1]{1,0:T(8,128)S(1)} %copy-done.3, f32[1,256]{1,0:T(1,128)S(1)} %copy-done.4, bf16[4,256,256]{2,1,0:T(8,128)(2,1)} %constant.37.clone.refs_3_.refs_2_.left_hbm, ...), custom_call_target="tpu_custom_call" | custom-call | flops 1342177280 | bytes 4194304 | tf_op jit(solution)/shard_map/first_parts/pallas_call | solution.py:205
  33.2 0.0 all-to-all-done.1
  33.2 0.1 collective-permute-start
  33.3 1.5 %collective-permute-done = bf16[8,4,16,256]{3,2,1,0:T(8,128)(2,1)S(1)} collective-permute-done((bf16[8,4,16,256]{3,2,1,0:T(8,128)(2,1)S(1)}, bf16[8,4,16,256]{3,2,1,0:T(8,128)(2,1)S(1)}, u32[]{:S(2)}, u32[]{:S(2)}) %collective-permute-start) | collective-permute-done | bytes 262176 | tf_op jit(solution)/shard_map/ppermute | solution.py:504
  34.8 0.1 pad_maximum_fusion.refs_6_
  34.9 7.5 %depth_steps.1 = (f32[8,9,16,128]{3,2,1,0:T(8,128)S(1)}, f32[8,9,16,128]{3,2,1,0:T(8,128)S(1)}, f32[2,256,256]{2,1,0:T(8,128)S(1)}, f32[256,256]{1,0:T(8,128)S(1)}, f32[256,256]{1,0:T(8,128)S(1)}) custom-call(s32[16]{0:T(128)S(1)} %copy-done.2, s32[1]{0:T(128)} %bitcast.refs_1_.place_ref, bf16[4,256,256]{2,1,0:T(8,128)(2,1)} %constant.37.clone.refs_3_.refs_2_.left_hbm, ...), custom_call_target="tpu_custom_call" | custom-call | flops 5368709120 | bytes 4194304 | tf_op jit(solution)/shard_map/depth_steps/pallas_call | solution.py:327
  42.5 0.2 collective-permute-start.1
  42.6 1.9 %collective-permute-done.1 = f32[8,9,16,128]{3,2,1,0:T(8,128)S(1)} collective-permute-done((f32[8,9,16,128]{3,2,1,0:T(8,128)S(1)}, f32[8,9,16,128]{3,2,1,0:T(8,128)S(1)}, u32[]{:S(2)}, u32[]{:S(2)}) %collective-permute-start.1) | collective-permute-done | bytes 589856 | tf_op jit(solution)/shard_map/ppermute | solution.py:504
  44.5 0.1 add.3
  44.6 0.1 fusion
  44.7 0.8 %pad_maximum_fusion.1 = f16[8,9,16,128]{3,2,1,0:T(8,128)(2,1)} fusion(f16[8,1,16,128]{3,2,1,0:T(8,128)(2,1)S(1)} %get-tuple-element.27, f16[8,8,16,128]{3,2,1,0:T(8,128)(2,1)S(1)} %fusion), kind=kLoop, calls=%fused_computation.5 | loop fusion | flops 147456 | bytes 589824 | tf_op jit(solution)/shard_map/concatenate | solution.py:550
  45.5 5.6 %all-to-all-start.2 = ((f16[8,9,16,128]{3,2,1,0:T(8,128)(2,1)}), f16[8,9,16,128]{3,2,1,0:T(8,128)(2,1)S(1)}, u32[]{:S(2)}, u32[]{:S(2)}) async-start(f16[8,9,16,128]{3,2,1,0:T(8,128)(2,1)} %pad_maximum_fusion.1), calls=%async_computation.2 | async-start | bytes 589824 | tf_op jit(solution)/shard_map/all_to_all | solution.py:551
  51.1 4.2 %last_field.1 = f32[2,256,256]{2,1,0:T(8,128)} custom-call(bf16[4,256,256]{2,1,0:T(8,128)(2,1)} %constant.37.clone.refs_3_.refs_2_.left_hbm, bf16[4,256,256]{2,1,0:T(8,128)(2,1)} %constant.38.clone.refs_4_.refs_3_.right_hbm, bf16[256,256]{1,0:T(8,128)(2,1)} %constant.35.clone.lanes_hbm.refs_5_.refs_6_.order_x_hbm.order_y_hbm, ...), custom_call_target="tpu_custom_call" | custom-call | flops 671088640 | bytes 4194304 | tf_op jit(solution)/shard_map/last_field/pallas_call | solution.py:372
  55.3 2.3 %all-to-all-done.2 = f16[8,9,16,128]{3,2,1,0:T(8,128)(2,1)S(1)} async-done(((f16[8,9,16,128]{3,2,1,0:T(8,128)(2,1)}), f16[8,9,16,128]{3,2,1,0:T(8,128)(2,1)S(1)}, u32[]{:S(2)}, u32[]{:S(2)}) %all-to-all-start.2) | async-done | bytes 294944 | tf_op jit(solution)/shard_map/all_to_all | solution.py:551
  57.7 0.8 %image_rows.1 = f32[4,16,256]{2,1,0:T(8,128)} custom-call(s32[1]{0:T(128)} %bitcast.refs_1_.place_ref, f32[128,128]{1,0:T(8,128)S(1)} %copy-done, f32[64,64]{1,0:T(8,128)S(1)} %copy-done.1, f32[8,9,16,128]{3,2,1,0:T(8,128)S(1)} %convert_element_type.28.share_ref), custom_call_target="tpu_custom_call" | custom-call | tf_op jit(solution)/shard_map/image_rows/pallas_call | solution.py:493
  (13 shorter events, 0.2 us)
Async XLA Ops:
  0.6 19.1 %copy-start.6 = (s32[4]{0:T(128)S(1)}, s32[4]{0:T(128)}, u32[]{:S(2)}) copy-start(s32[4]{0:T(128)} %param.21) | copy-start | bytes 52
  0.6 19.1 %copy-start.7 = (s32[16]{0:T(128)S(1)}, s32[16]{0:T(128)}, u32[]{:S(2)}) copy-start(s32[16]{0:T(128)} %constant.36.clone) | copy-start | bytes 196
  3.1 23.6 %copy-start.5 = (f32[2,10,4]{1,2,0:T(4,128)S(1)}, f32[2,10,4]{1,2,0:T(4,128)}, u32[]{:S(2)}) copy-start(f32[2,10,4]{1,2,0:T(4,128)} %param.19) | copy-start | bytes 964
  3.2 23.7 %copy-start.3 = (f32[256,1]{1,0:T(8,128)S(1)}, f32[256,1]{1,0:T(8,128)}, u32[]{:S(2)}) copy-start(f32[256,1]{1,0:T(8,128)} %constant.39.clone.refs_1_) | copy-start | bytes 3076
  3.2 23.7 %copy-start.4 = (f32[1,256]{1,0:T(1,128)S(1)}, f32[1,256]{1,0:T(1,128)}, u32[]{:S(2)}) copy-start(f32[1,256]{1,0:T(1,128)} %constant.40.clone.refs_2_) | copy-start | bytes 3076
  20.7 12.5 %all-to-all-start.1 = ((bf16[8,4,16,256]{3,2,1,0:T(8,128)(2,1)}), bf16[8,4,16,256]{3,2,1,0:T(8,128)(2,1)S(1)}, u32[]{:S(2)}, u32[]{:S(2)}) async-start(bf16[8,4,16,256]{3,2,1,0:T(8,128)(2,1)} %broadcast_in_dim.13), calls=%async_computation.1 | async-start | bytes 524288 | tf_op jit(solution)/shard_map/all_to_all | solution.py:534
  26.9 8.0 %copy-start.2 = (s32[16]{0:T(128)S(1)}, s32[16]{0:T(128)}, u32[]{:S(2)}) copy-start(s32[16]{0:T(128)} %refs_0_.2) | copy-start | bytes 196
  33.2 1.6 %collective-permute-start = (bf16[8,4,16,256]{3,2,1,0:T(8,128)(2,1)S(1)}, bf16[8,4,16,256]{3,2,1,0:T(8,128)(2,1)S(1)}, u32[]{:S(2)}, u32[]{:S(2)}) collective-permute-start(bf16[8,4,16,256]{3,2,1,0:T(8,128)(2,1)S(1)} %all-to-all-done.1), channel_id=1, source_target_pairs={{0,1},{1,0},{2,3},{3,2},{4,5},{5,4},{6,7},{7,6},{8,9},{9,8},{10,11... | collective-permute-start | bytes 786440 | tf_op jit(solution)/shard_map/ppermute | solution.py:504
  42.5 2.1 %collective-permute-start.1 = (f32[8,9,16,128]{3,2,1,0:T(8,128)S(1)}, f32[8,9,16,128]{3,2,1,0:T(8,128)S(1)}, u32[]{:S(2)}, u32[]{:S(2)}) collective-permute-start(f32[8,9,16,128]{3,2,1,0:T(8,128)S(1)} %get-tuple-element.18), channel_id=1, source_target_pairs={{0,1},{1,0},{2,3},{3,2},{4,5},{5,4},{6,7},{7,6},{8,9},{9,8},{10,11... | collective-permute-start | bytes 1769480 | tf_op jit(solution)/shard_map/ppermute | solution.py:504
  45.5 12.1 %all-to-all-start.2 = ((f16[8,9,16,128]{3,2,1,0:T(8,128)(2,1)}), f16[8,9,16,128]{3,2,1,0:T(8,128)(2,1)S(1)}, u32[]{:S(2)}, u32[]{:S(2)}) async-start(f16[8,9,16,128]{3,2,1,0:T(8,128)(2,1)} %pad_maximum_fusion.1), calls=%async_computation.2 | async-start | bytes 589824 | tf_op jit(solution)/shard_map/all_to_all | solution.py:551
  51.1 6.5 %copy-start = (f32[128,128]{1,0:T(8,128)S(1)}, f32[128,128]{1,0:T(8,128)}, u32[]{:S(2)}) copy-start(f32[128,128]{1,0:T(8,128)} %constant.41.clone.lanes_ref) | copy-start | bytes 196612
  51.1 6.5 %copy-start.1 = (f32[64,64]{1,0:T(8,128)S(1)}, f32[64,64]{1,0:T(8,128)}, u32[]{:S(2)}) copy-start(f32[64,64]{1,0:T(8,128)} %constant.42.clone.rows_ref) | copy-start | bytes 49156

commit v6 on v5

--- a/solution.py
+++ b/solution.py
@@ -545,11 +545,19 @@
         freq_slot, place, left, right, factors, parts, speed
     )
 
-    total = keep + swap_cores(send, devices)
-    power = jnp.ceil(jnp.log2(jnp.maximum(total[:, 2 * depth_count :], 1e-30)))
-    packed = jnp.concatenate([total[:, : 2 * depth_count] * jnp.exp2(-power), power], axis=1)
+    parts_end = 2 * depth_count
+
+    def pack(values, peak):
+        power = jnp.ceil(jnp.log2(jnp.maximum(peak, 1e-30)))
+        return jnp.concatenate([values * jnp.exp2(-power), power], axis=1).astype(jnp.float16)
+
+    swapped = swap_cores(pack(send[:, :parts_end], send[:, parts_end:]), devices).astype(jnp.float32)
+    peer_scale = jnp.exp2(swapped[:, parts_end:])
+    packed = pack(
+        keep[:, :parts_end] + swapped[:, :parts_end] * peer_scale, keep[:, parts_end:] + peer_scale
+    )
     shares = lax.all_to_all(
-        packed.astype(jnp.float16),
+        packed,
         "freq",
         split_axis=0,
         concat_axis=0,

time: 58.9 us -> 58.8 us (level)
  no operation moved by 1% of the time
where the time goes in v6:
time: 58.8 us; the launch traced here: 58.3 us
  Pallas kernels  21.2 us (36%)
  blocking collectives  16.4 us (28%)
  starting transfers between devices  11.9 us (20%)
  waiting for transfers between devices  5.27 us (9%)
  other arithmetic  1.43 us (2%)
  local copies, waits for them, and re-layouts  0.96 us (2%)
  between operations  0.87 us (1%)
    all_to_all x1, blocking collectives, on_device(): lax.all_to_all(spectra.astype(jnp.float16), 'freq', split_axis=0, concat_...  16.4 us
    pallas_call x1, Pallas kernels, depth_steps(): pl.pallas_call(kernel, out_shape=(share, share, jax.ShapeDtypeStruct((2,...  7.54 us
    pallas_call x1, Pallas kernels, first_parts(): pl.pallas_call(kernel, out_shape=(pltpu.VMEM(shape, jnp.float32), pltpu.H...  6.27 us
    all_to_all x1, starting transfers between devices, on_device(): lax.all_to_all(chosen, 'freq', split_axis=0, concat_axis=0, tiled=True, a...  6.01 us
    all_to_all x1, starting transfers between devices, on_device(): lax.all_to_all(packed, 'freq', split_axis=0, concat_axis=0, tiled=True, a...  5.64 us
    pallas_call x1, Pallas kernels, last_field(): pl.pallas_call(last_kernel, out_shape=jax.ShapeDtypeStruct((2, nx, ny), j...  4.16 us
    ppermute x2, waiting for transfers between devices, swap_cores(): return lax.ppermute(array, 'freq', [(i, i ^ 1) for i in range(count)])  2.98 us
    pallas_call x1, Pallas kernels, position_spectra(): pl.pallas_call(spectra_kernel, out_shape=jax.ShapeDtypeStruct((slots, 3,...  2.43 us
  transfers between devices with their start and end apart: 4, of which 3 were waited for; matrix products, arithmetic and copies ran while one was open for 0% of the time, Pallas kernels for 18%

profile of v6, /device:TPU:0, one launch (start us, length us, event | category | flops | bytes accessed | tf_op | source)
XLA Modules:
  0.0 58.3 jit_solution(9782312168033753873)
XLA Ops:
  0.6 0.0 copy-start.7
  0.7 2.4 %position_spectra.1 = f32[16,3,16,256]{3,2,1,0:T(8,128)S(1)} custom-call(s32[16]{0:T(128)} %refs_0_.2, bf16[32,256]{1,0:T(8,128)(2,1)} %constant.33.clone.table_hbm, bf16[16,256,256]{2,1,0:T(8,128)(2,1)} %traces_hbm.1, bf16[256,256]{1,0:T(8,128)(2,1)} %bitcast.30, bf16[256,256]{1,0:T(8,128)(2,1)} %constant.34.clone.rows_hbm, ...), custom_call_target="tpu_custom_call" | custom-call | flops 67108864 | bytes 2097152 | tf_op jit(solution)/shard_map/position_spectra/pallas_call | solution.py:440
  3.1 0.0 copy-start.5
  3.1 0.1 convert_element_type.27
  3.2 0.0 copy-start.3
  3.2 0.0 copy-start.4
  3.2 16.4 %all_to_all.15 = f16[16,3,16,256]{3,2,1,0:T(8,128)(2,1)S(1)} all-to-all(f16[16,3,16,256]{3,2,1,0:T(8,128)(2,1)S(1)} %convert_element_type.27), channel_id=1, replica_groups={{11,9,7,5,3,1,15,13,10,8,6,4,2,0,14,12},{27,25,23,21,19,17,31,29,26,24,..., dimensions={0} | all-to-all | bytes 786432 | tf_op jit(solution)/shard_map/all_to_all | solution.py:518
  19.7 0.2 convolution_convert_fusion
  20.0 0.7 %broadcast_in_dim.13 = bf16[8,4,16,256]{3,2,1,0:T(8,128)(2,1)} broadcast(bf16[4,16,256]{2,1,0:T(8,128)(2,1)S(1)} %bitcast.32), dimensions={1,2,3} | broadcast | bytes 294912 | tf_op jit(solution)/shard_map/broadcast_in_dim | solution.py:531
  20.7 6.0 %all-to-all-start.1 = ((bf16[8,4,16,256]{3,2,1,0:T(8,128)(2,1)}), bf16[8,4,16,256]{3,2,1,0:T(8,128)(2,1)S(1)}, u32[]{:S(2)}, u32[]{:S(2)}) async-start(bf16[8,4,16,256]{3,2,1,0:T(8,128)(2,1)} %broadcast_in_dim.13), calls=%async_computation.1 | async-start | bytes 524288 | tf_op jit(solution)/shard_map/all_to_all | solution.py:534
  26.7 0.1 copy.20.refs_0_
  26.8 0.1 multiply_bitcast_fusion
  26.9 0.0 copy-done.3
  26.9 0.0 copy-done.4
  26.9 0.0 copy-start.2
  27.0 6.3 %first_parts.1 = (f32[4,2,256,256]{3,2,1,0:T(8,128)S(1)}, f32[4,2,256,256]{3,2,1,0:T(8,128)}) custom-call(f32[2,10,4]{2,1,0:T(8,128)S(1)} %copy.20.refs_0_, f32[256,1]{1,0:T(8,128)S(1)} %copy-done.3, f32[1,256]{1,0:T(1,128)S(1)} %copy-done.4, bf16[4,256,256]{2,1,0:T(8,128)(2,1)} %constant.37.clone.refs_3_.refs_2_.left_hbm, ...), custom_call_target="tpu_custom_call" | custom-call | flops 1342177280 | bytes 4194304 | tf_op jit(solution)/shard_map/first_parts/pallas_call | solution.py:205
  33.2 0.0 all-to-all-done.1
  33.2 0.1 collective-permute-start
  33.3 1.5 %collective-permute-done = bf16[8,4,16,256]{3,2,1,0:T(8,128)(2,1)S(1)} collective-permute-done((bf16[8,4,16,256]{3,2,1,0:T(8,128)(2,1)S(1)}, bf16[8,4,16,256]{3,2,1,0:T(8,128)(2,1)S(1)}, u32[]{:S(2)}, u32[]{:S(2)}) %collective-permute-start) | collective-permute-done | bytes 262176 | tf_op jit(solution)/shard_map/ppermute | solution.py:504
  34.8 0.1 pad_maximum_fusion.refs_6_
  34.9 7.5 %depth_steps.1 = (f32[8,9,16,128]{3,2,1,0:T(8,128)S(1)}, f32[8,9,16,128]{3,2,1,0:T(8,128)S(1)}, f32[2,256,256]{2,1,0:T(8,128)S(1)}, f32[256,256]{1,0:T(8,128)S(1)}, f32[256,256]{1,0:T(8,128)S(1)}) custom-call(s32[16]{0:T(128)S(1)} %copy-done.2, s32[1]{0:T(128)} %bitcast.refs_1_.place_ref, bf16[4,256,256]{2,1,0:T(8,128)(2,1)} %constant.37.clone.refs_3_.refs_2_.left_hbm, ...), custom_call_target="tpu_custom_call" | custom-call | flops 5368709120 | bytes 4194304 | tf_op jit(solution)/shard_map/depth_steps/pallas_call | solution.py:327
  42.5 0.1 multiply_convert_fusion
  42.6 0.1 pad_maximum_fusion.1
  42.6 0.2 collective-permute-start.1
  42.8 1.5 %collective-permute-done.1 = f16[8,9,16,128]{3,2,1,0:T(8,128)(2,1)S(1)} collective-permute-done((f16[8,9,16,128]{3,2,1,0:T(8,128)(2,1)S(1)}, f16[8,9,16,128]{3,2,1,0:T(8,128)(2,1)S(1)}, u32[]{:S(2)}, u32[]{:S(2)}) %collective-permute-start.1) | collective-permute-done | bytes 294944 | tf_op jit(solution)/shard_map/ppermute | solution.py:504
  44.3 0.1 exponential_bitcast_fusion
  44.4 0.1 fusion.2
  44.5 0.8 %pad_maximum_fusion.2 = f16[8,9,16,128]{3,2,1,0:T(8,128)(2,1)} fusion(f16[8,1,16,128]{3,2,1,0:T(8,128)(2,1)S(1)} %get-tuple-element.27, f16[8,8,16,128]{3,2,1,0:T(8,128)(2,1)S(1)} %fusion.2), kind=kLoop, calls=%fused_computation.9 | loop fusion | flops 147456 | bytes 589824 | tf_op jit(solution)/shard_map/concatenate | solution.py:552
  45.3 5.6 %all-to-all-start.2 = ((f16[8,9,16,128]{3,2,1,0:T(8,128)(2,1)}), f16[8,9,16,128]{3,2,1,0:T(8,128)(2,1)S(1)}, u32[]{:S(2)}, u32[]{:S(2)}) async-start(f16[8,9,16,128]{3,2,1,0:T(8,128)(2,1)} %pad_maximum_fusion.2), calls=%async_computation.2 | async-start | bytes 589824 | tf_op jit(solution)/shard_map/all_to_all | solution.py:559
  51.0 4.2 %last_field.1 = f32[2,256,256]{2,1,0:T(8,128)} custom-call(bf16[4,256,256]{2,1,0:T(8,128)(2,1)} %constant.37.clone.refs_3_.refs_2_.left_hbm, bf16[4,256,256]{2,1,0:T(8,128)(2,1)} %constant.38.clone.refs_4_.refs_3_.right_hbm, bf16[256,256]{1,0:T(8,128)(2,1)} %constant.35.clone.lanes_hbm.refs_5_.refs_6_.order_x_hbm.order_y_hbm, ...), custom_call_target="tpu_custom_call" | custom-call | flops 671088640 | bytes 4194304 | tf_op jit(solution)/shard_map/last_field/pallas_call | solution.py:372
  55.1 2.3 %all-to-all-done.2 = f16[8,9,16,128]{3,2,1,0:T(8,128)(2,1)S(1)} async-done(((f16[8,9,16,128]{3,2,1,0:T(8,128)(2,1)}), f16[8,9,16,128]{3,2,1,0:T(8,128)(2,1)S(1)}, u32[]{:S(2)}, u32[]{:S(2)}) %all-to-all-start.2) | async-done | bytes 294944 | tf_op jit(solution)/shard_map/all_to_all | solution.py:559
  57.5 0.8 %image_rows.1 = f32[4,16,256]{2,1,0:T(8,128)} custom-call(s32[1]{0:T(128)} %bitcast.refs_1_.place_ref, f32[128,128]{1,0:T(8,128)S(1)} %copy-done, f32[64,64]{1,0:T(8,128)S(1)} %copy-done.1, f32[8,9,16,128]{3,2,1,0:T(8,128)S(1)} %convert_element_type.33.share_ref), custom_call_target="tpu_custom_call" | custom-call | tf_op jit(solution)/shard_map/image_rows/pallas_call | solution.py:493
  (16 shorter events, 0.2 us)
Async XLA Ops:
  0.6 19.1 %copy-start.6 = (s32[4]{0:T(128)S(1)}, s32[4]{0:T(128)}, u32[]{:S(2)}) copy-start(s32[4]{0:T(128)} %param.21) | copy-start | bytes 52
  0.6 19.1 %copy-start.7 = (s32[16]{0:T(128)S(1)}, s32[16]{0:T(128)}, u32[]{:S(2)}) copy-start(s32[16]{0:T(128)} %constant.36.clone) | copy-start | bytes 196
  3.1 23.6 %copy-start.5 = (f32[2,10,4]{1,2,0:T(4,128)S(1)}, f32[2,10,4]{1,2,0:T(4,128)}, u32[]{:S(2)}) copy-start(f32[2,10,4]{1,2,0:T(4,128)} %param.19) | copy-start | bytes 964
  3.2 23.7 %copy-start.3 = (f32[256,1]{1,0:T(8,128)S(1)}, f32[256,1]{1,0:T(8,128)}, u32[]{:S(2)}) copy-start(f32[256,1]{1,0:T(8,128)} %constant.39.clone.refs_1_) | copy-start | bytes 3076
  3.2 23.7 %copy-start.4 = (f32[1,256]{1,0:T(1,128)S(1)}, f32[1,256]{1,0:T(1,128)}, u32[]{:S(2)}) copy-start(f32[1,256]{1,0:T(1,128)} %constant.40.clone.refs_2_) | copy-start | bytes 3076
  20.7 12.5 %all-to-all-start.1 = ((bf16[8,4,16,256]{3,2,1,0:T(8,128)(2,1)}), bf16[8,4,16,256]{3,2,1,0:T(8,128)(2,1)S(1)}, u32[]{:S(2)}, u32[]{:S(2)}) async-start(bf16[8,4,16,256]{3,2,1,0:T(8,128)(2,1)} %broadcast_in_dim.13), calls=%async_computation.1 | async-start | bytes 524288 | tf_op jit(solution)/shard_map/all_to_all | solution.py:534
  26.9 8.0 %copy-start.2 = (s32[16]{0:T(128)S(1)}, s32[16]{0:T(128)}, u32[]{:S(2)}) copy-start(s32[16]{0:T(128)} %refs_0_.2) | copy-start | bytes 196
  33.2 1.6 %collective-permute-start = (bf16[8,4,16,256]{3,2,1,0:T(8,128)(2,1)S(1)}, bf16[8,4,16,256]{3,2,1,0:T(8,128)(2,1)S(1)}, u32[]{:S(2)}, u32[]{:S(2)}) collective-permute-start(bf16[8,4,16,256]{3,2,1,0:T(8,128)(2,1)S(1)} %all-to-all-done.1), channel_id=1, source_target_pairs={{0,1},{1,0},{2,3},{3,2},{4,5},{5,4},{6,7},{7,6},{8,9},{9,8},{10,11... | collective-permute-start | bytes 786440 | tf_op jit(solution)/shard_map/ppermute | solution.py:504
  42.6 1.6 %collective-permute-start.1 = (f16[8,9,16,128]{3,2,1,0:T(8,128)(2,1)S(1)}, f16[8,9,16,128]{3,2,1,0:T(8,128)(2,1)S(1)}, u32[]{:S(2)}, u32[]{:S(2)}) collective-permute-start(f16[8,9,16,128]{3,2,1,0:T(8,128)(2,1)S(1)} %pad_maximum_fusion.1), channel_id=1, source_target_pairs={{0,1},{1,0},{2,3},{3,2},{4,5},{5,4},{6,7},{7,6},{8,9},{9,8},{10,11... | collective-permute-start | bytes 884744 | tf_op jit(solution)/shard_map/ppermute | solution.py:504
  45.3 12.1 %all-to-all-start.2 = ((f16[8,9,16,128]{3,2,1,0:T(8,128)(2,1)}), f16[8,9,16,128]{3,2,1,0:T(8,128)(2,1)S(1)}, u32[]{:S(2)}, u32[]{:S(2)}) async-start(f16[8,9,16,128]{3,2,1,0:T(8,128)(2,1)} %pad_maximum_fusion.2), calls=%async_computation.2 | async-start | bytes 589824 | tf_op jit(solution)/shard_map/all_to_all | solution.py:559
  51.0 6.5 %copy-start = (f32[128,128]{1,0:T(8,128)S(1)}, f32[128,128]{1,0:T(8,128)}, u32[]{:S(2)}) copy-start(f32[128,128]{1,0:T(8,128)} %constant.41.clone.lanes_ref) | copy-start | bytes 196612
  51.0 6.5 %copy-start.1 = (f32[64,64]{1,0:T(8,128)S(1)}, f32[64,64]{1,0:T(8,128)}, u32[]{:S(2)}) copy-start(f32[64,64]{1,0:T(8,128)} %constant.42.clone.rows_ref) | copy-start | bytes 49156
